TPU v7x, 512 devices: a whole 4x8x8 slice. The times are simulated.
512 devices in a mesh: cable: 32 (over y, x), pair: 16 (over z, core).
Axes of the slice: x: 4, y: 8, z: 8, core: 2. Of those that a mesh axis runs over, the one named last changes fastest.
Arguments:
- raw_strain: bfloat16 [4096, 2048], P('cable', 'pair'), may hold values from -40 to 40
- smooth_taps: float32 [101], replicated, may hold values from 0.02 to 1
- partner_block: int32 [32, 16], P('cable'), may hold values from 0 to 31, as said below
- chan_offset: int32 [32, 16], P('cable'), may hold values from 0 to 127
- pair_count: int32 [32], P('cable'), may hold values from 1 to 16
Outputs:
- correlations: float32 [32, 16, 401, 128], P('cable', 'pair')
Inputs may be any that keep to these rules, and one draw needn't show every extreme that they name: `partner_block`: each entry lies within 2 of its row's block index.
All inputs are finite; a program needn't handle non-finite values.
Results may differ from a plain program's by a relative error of at most 0.014.
Values may be sent and summed in bfloat16 or wider, within the bound.
No kernel may reach another device: no remote copies, remote signals or barrier semaphores. Data moves between devices by JAX's collectives and lax.ppermute only.
A program may use at most 64 MiB of HBM per device.

v0:
```python
import math

import jax
import jax.numpy as jnp
from jax import lax
from jax.sharding import PartitionSpec as P

LAG = 200
REACH = 2


EPSILON = 1e-05


def from_behind(value, axis, steps):
    count = lax.axis_size(axis)
    first, last = (max(0, -steps), min(count, count - steps))
    return lax.ppermute(value, axis, [(source, source + steps) for source in range(first, last)])


def extended_2(value, sides, width):
    for axis, dim in sides:
        devices, length = (lax.axis_size(axis), value.shape[dim])
        up = [(i, (i + 1) % devices) for i in range(devices - 1)]
        down = [(j, i) for i, j in up]
        last = lax.slice_in_dim(value, length - width, length, axis=dim)
        first = lax.slice_in_dim(value, 0, width, axis=dim)
        before = lax.ppermute(last, axis, up)
        after = lax.ppermute(first, axis, down)
        value = jnp.concatenate([before, value, after], axis=dim)
    return value


def split_pair(table):
    upper = table.astype(jnp.bfloat16)
    lower = (table - upper.astype(jnp.float32)).astype(jnp.bfloat16)
    return (upper, lower)


def envelope_units(raw_strain, smooth_taps, extended):
    magnitude = jnp.abs(extended)[:, None, :]
    taps_upper, taps_lower = split_pair(smooth_taps)
    smoothed = lax.conv_general_dilated(
        magnitude, taps_upper[None, None, :], (1,), "VALID", preferred_element_type=jnp.float32
    )[:, 0, :]
    smoothed = (
        smoothed
        + lax.conv_general_dilated(
            magnitude, taps_lower[None, None, :], (1,), "VALID", preferred_element_type=jnp.float32
        )[:, 0, :]
    )
    envelope = smoothed / jnp.sum(smooth_taps)
    return (raw_strain.astype(jnp.float32) / (envelope + EPSILON)).astype(jnp.bfloat16)


def split_product(series, table):
    upper, lower = split_pair(table)
    return jnp.dot(series, upper, preferred_element_type=jnp.float32) + jnp.dot(
        series, lower, preferred_element_type=jnp.float32
    )


def split_einsum(table, spectrum):
    table_upper, table_lower = split_pair(table)
    spec_upper, spec_lower = split_pair(spectrum)
    total = jnp.einsum("lk,sak->sla", table_upper, spec_upper, preferred_element_type=jnp.float32)
    total = total + jnp.einsum(
        "lk,sak->sla", table_upper, spec_lower, preferred_element_type=jnp.float32
    )
    return total + jnp.einsum(
        "lk,sak->sla", table_lower, spec_upper, preferred_element_type=jnp.float32
    )


def correlate(own_series, partners, max_lag):
    channels, length = own_series.shape
    slot_count = partners.shape[0]
    fft_length = ((length + max_lag) // 512 + 1) * 512
    half_length = fft_length // 2
    freq_blocks = half_length // 256
    lag_count = 2 * max_lag + 1
    stacked = jnp.concatenate([own_series[None], partners], 0).reshape(
        (slot_count + 1) * channels, length
    )
    time_index = jnp.arange(length, dtype=jnp.int32)
    shifts = (jnp.arange(lag_count, dtype=jnp.int32) - max_lag) % fft_length
    alternating = jnp.where(time_index % 2 == 0, 1.0, -1.0).astype(jnp.bfloat16)
    nyquist = jnp.dot(stacked, alternating, preferred_element_type=jnp.float32).reshape(
        slot_count + 1, channels
    )
    nyquist_product = nyquist[0][None] * nyquist[1:]
    lag_sign = jnp.where(shifts % 2 == 0, 1.0, -1.0).astype(jnp.float32) / fft_length
    initial = lag_sign[None, :, None] * nyquist_product[:, None, :]

    def add_block(block_id, running):
        frequencies = block_id * 256 + jnp.arange(256, dtype=jnp.int32)
        forward = (
            2.0
            * math.pi
            / fft_length
            * (time_index[:, None] * frequencies[None, :] % fft_length).astype(jnp.float32)
        )
        cosine_part = split_product(stacked, jnp.cos(forward)).reshape(
            slot_count + 1, channels, 256
        )
        sine_part = split_product(stacked, jnp.sin(forward)).reshape(slot_count + 1, channels, 256)
        real_part = cosine_part[0] * cosine_part[1:] + sine_part[0] * sine_part[1:]
        imag_part = sine_part[0] * cosine_part[1:] - cosine_part[0] * sine_part[1:]
        weights = jnp.where(frequencies == 0, 1.0, 2.0).astype(jnp.float32) / fft_length
        backward = (
            2.0
            * math.pi
            / fft_length
            * (shifts[:, None] * frequencies[None, :] % fft_length).astype(jnp.float32)
        )
        real_term = split_einsum(jnp.cos(backward) * weights[None, :], real_part)
        imag_term = split_einsum(jnp.sin(backward) * weights[None, :], imag_part)
        return running + real_term - imag_term

    return lax.fori_loop(0, freq_blocks, add_block, initial)


def step_block(series, direction):
    return from_behind(series, "cable", direction)


def per_device(raw_strain, smooth_taps, partner_block, chan_offset, pair_count):
    block_rows, slice_length = raw_strain.shape
    half_window = (smooth_taps.shape[0] - 1) // 2
    extended = extended_2(raw_strain, (("pair", 1),), half_window)
    unit_series = envelope_units(raw_strain, smooth_taps, extended)
    cable_place = lax.axis_index("cable")
    pair_place = lax.axis_index("pair")
    pair_width = lax.axis_size("pair")
    lower_pieces = []
    current = unit_series
    for hop_count in range(REACH):
        current = step_block(current, 1)
        lower_pieces.append(current)
    upper_pieces = []
    current = unit_series
    for hop_count in range(REACH + 1):
        current = step_block(current, -1)
        upper_pieces.append(current)
    window = jnp.concatenate(lower_pieces[::-1] + [unit_series] + upper_pieces, 0)
    slot_total = partner_block.shape[1]
    slots_here = slot_total // pair_width
    row_starts = (partner_block[0] - cable_place + REACH) * block_rows + chan_offset[0]
    first_slot = pair_place * slots_here
    whole_window = lax.all_gather(window, "pair", axis=1, tiled=True)
    own_series = whole_window[REACH * block_rows : (REACH + 1) * block_rows]
    my_starts = lax.dynamic_slice_in_dim(row_starts, first_slot, slots_here, 0)
    partners = jnp.stack([lax.dynamic_slice_in_dim(whole_window, my_starts[0], block_rows, 0)], 0)
    values = correlate(own_series, partners, LAG)
    slot_ids = first_slot + jnp.arange(slots_here, dtype=jnp.int32)
    live_slots = (slot_ids < pair_count[0]).astype(jnp.float32)
    scaled = values * (live_slots[:, None, None] / math.sqrt(own_series.shape[1]))
    return scaled[None]


def solution(mesh):
    in_specs = (P("cable", "pair"), P(), P("cable", None), P("cable", None), P("cable"))
    out_specs = P("cable", "pair", None, None)
    return jax.shard_map(
        per_device, mesh=mesh, in_specs=in_specs, out_specs=out_specs, check_vma=False
    )
```

profile of v0, /device:TPU:1, one launch (start us, length us, event | category | flops | bytes accessed | tf_op | source)
XLA Modules:
  0.0 339.2 jit_solution(2738193848740347981)
XLA Ops:
  7.4 5.4 %collective-permute-start = (bf16[128,50]{0,1:T(8,128)(2,1)S(1)}, bf16[128,50]{0,1:T(8,128)(2,1)S(1)}, u32[]{:S(2)}, u32[]{:S(2)}) collective-permute-start(bf16[128,50]{0,1:T(8,128)(2,1)S(1)} %get-tuple-element.158), channel_id=1, source_target_pairs={{0,1},{1,2},{2,3},{3,4},{4,5},{5,6},{6,7},{7,8},{8,9},{9,10},{10,1... | collective-permute-start | bytes 38408 | tf_op jit(solution)/shard_map/ppermute | solution.py:28
  12.8 4.7 %collective-permute-start.1 = (bf16[128,50]{0,1:T(8,128)(2,1)S(1)}, bf16[128,50]{0,1:T(8,128)(2,1)S(1)}, u32[]{:S(2)}, u32[]{:S(2)}) collective-permute-start(bf16[128,50]{0,1:T(8,128)(2,1)S(1)} %get-tuple-element.159), channel_id=1, source_target_pairs={{1,0},{2,1},{3,2},{4,3},{5,4},{6,5},{7,6},{8,7},{9,8},{10,9},{11,1... | collective-permute-start | bytes 38408 | tf_op jit(solution)/shard_map/ppermute | solution.py:29
  20.3 2.7 fusion.118
  23.0 3.4 fusion.106
  29.0 4.0 %collective-permute-start.3 = (bf16[128,128]{0,1:T(8,128)(2,1)S(1)}, bf16[128,128]{0,1:T(8,128)(2,1)S(1)}, u32[]{:S(2)}, u32[]{:S(2)}) collective-permute-start(bf16[128,128]{0,1:T(8,128)(2,1)S(1)} %collective-permute-done.2), channel_id=1, source_target_pairs={{0,16},{16,32},{32,48},{48,64},{64,80},{80,96},{96,112},{112,128},... | collective-permute-start | bytes 98312 | tf_op jit(solution)/shard_map/ppermute | solution.py:18
  34.4 3.3 collective-permute-done.5
  39.0 3.3 collective-permute-done.6
  46.5 57.4 %all-gather.2.cloned.1.call-done = bf16[768,2048]{0,1:T(8,128)(2,1)} async-done(((bf16[768,128]{0,1:T(8,128)(2,1)}), bf16[768,2048]{0,1:T(8,128)(2,1)}) %all-gather.2.cloned.1.call-update) | async-done | bytes 3145744 | tf_op jit(solution)/shard_map/all_gather | solution.py:150
  106.8 224.3 %while.16 = (s32[]{:T(128)}, f32[1,401,128]{2,1,0:T(8,128)S(1)}, bf16[256,2048]{1,0:T(8,128)(2,1)S(1)}, s32[]{:T(128)}, s32[]{:T(128)}) while((s32[]{:T(128)}, f32[1,401,128]{2,1,0:T(8,128)S(1)}, bf16[256,2048]{1,0:T(8,128)(2,1)S(1)}, s32[]{:T(128)}, s32[]{:T(128)}) %tuple.51), condition=%wide.region_2.3_spmd.clone, body=%wide.region_1.2_spmd.clone.sunk | while | flops 1263962880 | bytes 9833517 | solution.py:120
  107.1 8.2 %fusion.172 = f32[256,256]{1,0:T(8,128)S(1)} fusion(bf16[256,2048]{1,0:T(8,128)(2,1)S(1)} %get-tuple-element.198, s32[256]{0:T(256)S(1)} %iota_add_fusion.2), kind=kOutput, calls=%fused_computation.34.clone.1 | convolution fusion | flops 273678336 | bytes 1311744 | tf_op jit(solution)/shard_map/while/body/eval_jaxpr/dot_general | solution.py:58
  115.2 8.8 %fusion.173 = f32[256,256]{0,1:T(8,128)S(1)} fusion(f32[256,256]{1,0:T(8,128)S(1)} %fusion.172, bf16[256,2048]{1,0:T(8,128)(2,1)S(1)} %get-tuple-element.198, s32[256]{0:T(256)S(1)} %iota_add_fusion.2), kind=kOutput, calls=%fused_computation.19.clone.1 | convolution fusion | flops 275316736 | bytes 1573888 | tf_op jit(solution)/shard_map/while/body/eval_jaxpr/dot_general | solution.py:58
  124.0 8.3 %fusion.174 = f32[256,256]{1,0:T(8,128)S(1)} fusion(bf16[256,2048]{1,0:T(8,128)(2,1)S(1)} %get-tuple-element.198, s32[256]{0:T(256)S(1)} %iota_add_fusion.2), kind=kOutput, calls=%fused_computation.35.clone.1 | convolution fusion | flops 273678336 | bytes 1311744 | tf_op jit(solution)/shard_map/while/body/eval_jaxpr/dot_general | solution.py:58
  132.3 8.2 %fusion.175 = f32[256,256]{0,1:T(8,128)S(1)} fusion(f32[256,256]{1,0:T(8,128)S(1)} %fusion.174, bf16[256,2048]{1,0:T(8,128)(2,1)S(1)} %get-tuple-element.198, s32[256]{0:T(256)S(1)} %iota_add_fusion.2), kind=kOutput, calls=%fused_computation.21.clone.1 | convolution fusion | flops 275316736 | bytes 1573888 | tf_op jit(solution)/shard_map/while/body/eval_jaxpr/dot_general | solution.py:58
  142.3 2.0 convolution_add_fusion.10
  146.1 1.8 convolution_add_fusion.9
  147.9 1.8 fusion.177
  149.7 1.8 fusion.179
  151.9 8.2 %fusion.172 = f32[256,256]{1,0:T(8,128)S(1)} fusion(bf16[256,2048]{1,0:T(8,128)(2,1)S(1)} %get-tuple-element.198, s32[256]{0:T(256)S(1)} %iota_add_fusion.2), kind=kOutput, calls=%fused_computation.34.clone.1 | convolution fusion | flops 273678336 | bytes 1311744 | tf_op jit(solution)/shard_map/while/body/eval_jaxpr/dot_general | solution.py:58
  160.1 8.4 %fusion.173 = f32[256,256]{0,1:T(8,128)S(1)} fusion(f32[256,256]{1,0:T(8,128)S(1)} %fusion.172, bf16[256,2048]{1,0:T(8,128)(2,1)S(1)} %get-tuple-element.198, s32[256]{0:T(256)S(1)} %iota_add_fusion.2), kind=kOutput, calls=%fused_computation.19.clone.1 | convolution fusion | flops 275316736 | bytes 1573888 | tf_op jit(solution)/shard_map/while/body/eval_jaxpr/dot_general | solution.py:58
  168.5 8.3 %fusion.174 = f32[256,256]{1,0:T(8,128)S(1)} fusion(bf16[256,2048]{1,0:T(8,128)(2,1)S(1)} %get-tuple-element.198, s32[256]{0:T(256)S(1)} %iota_add_fusion.2), kind=kOutput, calls=%fused_computation.35.clone.1 | convolution fusion | flops 273678336 | bytes 1311744 | tf_op jit(solution)/shard_map/while/body/eval_jaxpr/dot_general | solution.py:58
  176.8 8.2 %fusion.175 = f32[256,256]{0,1:T(8,128)S(1)} fusion(f32[256,256]{1,0:T(8,128)S(1)} %fusion.174, bf16[256,2048]{1,0:T(8,128)(2,1)S(1)} %get-tuple-element.198, s32[256]{0:T(256)S(1)} %iota_add_fusion.2), kind=kOutput, calls=%fused_computation.21.clone.1 | convolution fusion | flops 275316736 | bytes 1573888 | tf_op jit(solution)/shard_map/while/body/eval_jaxpr/dot_general | solution.py:58
  186.8 2.2 convolution_add_fusion.10
  190.8 1.8 convolution_add_fusion.9
  192.6 1.8 fusion.177
  194.4 1.8 fusion.179
  196.4 8.2 %fusion.172 = f32[256,256]{1,0:T(8,128)S(1)} fusion(bf16[256,2048]{1,0:T(8,128)(2,1)S(1)} %get-tuple-element.198, s32[256]{0:T(256)S(1)} %iota_add_fusion.2), kind=kOutput, calls=%fused_computation.34.clone.1 | convolution fusion | flops 273678336 | bytes 1311744 | tf_op jit(solution)/shard_map/while/body/eval_jaxpr/dot_general | solution.py:58
  204.6 8.4 %fusion.173 = f32[256,256]{0,1:T(8,128)S(1)} fusion(f32[256,256]{1,0:T(8,128)S(1)} %fusion.172, bf16[256,2048]{1,0:T(8,128)(2,1)S(1)} %get-tuple-element.198, s32[256]{0:T(256)S(1)} %iota_add_fusion.2), kind=kOutput, calls=%fused_computation.19.clone.1 | convolution fusion | flops 275316736 | bytes 1573888 | tf_op jit(solution)/shard_map/while/body/eval_jaxpr/dot_general | solution.py:58
  213.0 8.5 %fusion.174 = f32[256,256]{1,0:T(8,128)S(1)} fusion(bf16[256,2048]{1,0:T(8,128)(2,1)S(1)} %get-tuple-element.198, s32[256]{0:T(256)S(1)} %iota_add_fusion.2), kind=kOutput, calls=%fused_computation.35.clone.1 | convolution fusion | flops 273678336 | bytes 1311744 | tf_op jit(solution)/shard_map/while/body/eval_jaxpr/dot_general | solution.py:58
  221.5 8.2 %fusion.175 = f32[256,256]{0,1:T(8,128)S(1)} fusion(f32[256,256]{1,0:T(8,128)S(1)} %fusion.174, bf16[256,2048]{1,0:T(8,128)(2,1)S(1)} %get-tuple-element.198, s32[256]{0:T(256)S(1)} %iota_add_fusion.2), kind=kOutput, calls=%fused_computation.21.clone.1 | convolution fusion | flops 275316736 | bytes 1573888 | tf_op jit(solution)/shard_map/while/body/eval_jaxpr/dot_general | solution.py:58
  231.6 2.0 convolution_add_fusion.10
  235.3 1.8 convolution_add_fusion.9
  237.1 1.8 fusion.177
  238.9 1.8 fusion.179
  240.9 8.2 %fusion.172 = f32[256,256]{1,0:T(8,128)S(1)} fusion(bf16[256,2048]{1,0:T(8,128)(2,1)S(1)} %get-tuple-element.198, s32[256]{0:T(256)S(1)} %iota_add_fusion.2), kind=kOutput, calls=%fused_computation.34.clone.1 | convolution fusion | flops 273678336 | bytes 1311744 | tf_op jit(solution)/shard_map/while/body/eval_jaxpr/dot_general | solution.py:58
  249.1 8.6 %fusion.173 = f32[256,256]{0,1:T(8,128)S(1)} fusion(f32[256,256]{1,0:T(8,128)S(1)} %fusion.172, bf16[256,2048]{1,0:T(8,128)(2,1)S(1)} %get-tuple-element.198, s32[256]{0:T(256)S(1)} %iota_add_fusion.2), kind=kOutput, calls=%fused_computation.19.clone.1 | convolution fusion | flops 275316736 | bytes 1573888 | tf_op jit(solution)/shard_map/while/body/eval_jaxpr/dot_general | solution.py:58
  257.7 8.3 %fusion.174 = f32[256,256]{1,0:T(8,128)S(1)} fusion(bf16[256,2048]{1,0:T(8,128)(2,1)S(1)} %get-tuple-element.198, s32[256]{0:T(256)S(1)} %iota_add_fusion.2), kind=kOutput, calls=%fused_computation.35.clone.1 | convolution fusion | flops 273678336 | bytes 1311744 | tf_op jit(solution)/shard_map/while/body/eval_jaxpr/dot_general | solution.py:58
  266.0 8.2 %fusion.175 = f32[256,256]{0,1:T(8,128)S(1)} fusion(f32[256,256]{1,0:T(8,128)S(1)} %fusion.174, bf16[256,2048]{1,0:T(8,128)(2,1)S(1)} %get-tuple-element.198, s32[256]{0:T(256)S(1)} %iota_add_fusion.2), kind=kOutput, calls=%fused_computation.21.clone.1 | convolution fusion | flops 275316736 | bytes 1573888 | tf_op jit(solution)/shard_map/while/body/eval_jaxpr/dot_general | solution.py:58
  276.0 2.0 convolution_add_fusion.10
  279.8 1.8 convolution_add_fusion.9
  281.6 1.8 fusion.177
  283.4 1.8 fusion.179
  285.7 8.2 %fusion.172 = f32[256,256]{1,0:T(8,128)S(1)} fusion(bf16[256,2048]{1,0:T(8,128)(2,1)S(1)} %get-tuple-element.198, s32[256]{0:T(256)S(1)} %iota_add_fusion.2), kind=kOutput, calls=%fused_computation.34.clone.1 | convolution fusion | flops 273678336 | bytes 1311744 | tf_op jit(solution)/shard_map/while/body/eval_jaxpr/dot_general | solution.py:58
  293.8 8.4 %fusion.173 = f32[256,256]{0,1:T(8,128)S(1)} fusion(f32[256,256]{1,0:T(8,128)S(1)} %fusion.172, bf16[256,2048]{1,0:T(8,128)(2,1)S(1)} %get-tuple-element.198, s32[256]{0:T(256)S(1)} %iota_add_fusion.2), kind=kOutput, calls=%fused_computation.19.clone.1 | convolution fusion | flops 275316736 | bytes 1573888 | tf_op jit(solution)/shard_map/while/body/eval_jaxpr/dot_general | solution.py:58
  302.2 8.3 %fusion.174 = f32[256,256]{1,0:T(8,128)S(1)} fusion(bf16[256,2048]{1,0:T(8,128)(2,1)S(1)} %get-tuple-element.198, s32[256]{0:T(256)S(1)} %iota_add_fusion.2), kind=kOutput, calls=%fused_computation.35.clone.1 | convolution fusion | flops 273678336 | bytes 1311744 | tf_op jit(solution)/shard_map/while/body/eval_jaxpr/dot_general | solution.py:58
  310.6 8.2 %fusion.175 = f32[256,256]{0,1:T(8,128)S(1)} fusion(f32[256,256]{1,0:T(8,128)S(1)} %fusion.174, bf16[256,2048]{1,0:T(8,128)(2,1)S(1)} %get-tuple-element.198, s32[256]{0:T(256)S(1)} %iota_add_fusion.2), kind=kOutput, calls=%fused_computation.21.clone.1 | convolution fusion | flops 275316736 | bytes 1573888 | tf_op jit(solution)/shard_map/while/body/eval_jaxpr/dot_general | solution.py:58
  320.6 2.2 convolution_add_fusion.10
  326.3 1.8 fusion.177
  328.1 1.8 fusion.179
  (77 shorter events, 33.9 us)
Async XLA Ops:
  6.5 97.3 %all-gather.2.cloned.1.call-start = ((), (), s32[]{:S(2)}) async-start(), calls=%async_computation | async-start | bytes 3342336 | tf_op jit(solution)/shard_map/all_gather | solution.py:150
  7.4 12.6 %collective-permute-start = (bf16[128,50]{0,1:T(8,128)(2,1)S(1)}, bf16[128,50]{0,1:T(8,128)(2,1)S(1)}, u32[]{:S(2)}, u32[]{:S(2)}) collective-permute-start(bf16[128,50]{0,1:T(8,128)(2,1)S(1)} %get-tuple-element.158), channel_id=1, source_target_pairs={{0,1},{1,2},{2,3},{3,4},{4,5},{5,6},{6,7},{7,8},{8,9},{9,10},{10,1... | collective-permute-start | bytes 38408 | tf_op jit(solution)/shard_map/ppermute | solution.py:28
  12.8 7.2 %collective-permute-start.1 = (bf16[128,50]{0,1:T(8,128)(2,1)S(1)}, bf16[128,50]{0,1:T(8,128)(2,1)S(1)}, u32[]{:S(2)}, u32[]{:S(2)}) collective-permute-start(bf16[128,50]{0,1:T(8,128)(2,1)S(1)} %get-tuple-element.159), channel_id=1, source_target_pairs={{1,0},{2,1},{3,2},{4,3},{5,4},{6,5},{7,6},{8,7},{9,8},{10,9},{11,1... | collective-permute-start | bytes 38408 | tf_op jit(solution)/shard_map/ppermute | solution.py:29
  23.0 20.1 %copy-start.1 = (s32[1,16]{1,0:T(1,128)S(1)}, s32[1,16]{1,0:T(1,128)}, u32[]{:S(2)}) copy-start(s32[1,16]{1,0:T(1,128)} %param.10) | copy-start | bytes 196
  23.0 20.1 %copy-start.2 = (s32[1,16]{1,0:T(1,128)S(1)}, s32[1,16]{1,0:T(1,128)}, u32[]{:S(2)}) copy-start(s32[1,16]{1,0:T(1,128)} %param.9) | copy-start | bytes 196
  26.4 2.6 collective-permute-start.2
  27.7 5.3 %collective-permute-start.4 = (bf16[128,128]{0,1:T(8,128)(2,1)S(1)}, bf16[128,128]{0,1:T(8,128)(2,1)S(1)}, u32[]{:S(2)}, u32[]{:S(2)}) collective-permute-start(bf16[128,128]{0,1:T(8,128)(2,1)S(1)} %divide_convert_fusion), channel_id=1, source_target_pairs={{16,0},{32,16},{48,32},{64,48},{80,64},{96,80},{112,96},{128,112},... | collective-permute-start | bytes 98312 | tf_op jit(solution)/shard_map/ppermute | solution.py:18
  29.0 5.3 %collective-permute-start.3 = (bf16[128,128]{0,1:T(8,128)(2,1)S(1)}, bf16[128,128]{0,1:T(8,128)(2,1)S(1)}, u32[]{:S(2)}, u32[]{:S(2)}) collective-permute-start(bf16[128,128]{0,1:T(8,128)(2,1)S(1)} %collective-permute-done.2), channel_id=1, source_target_pairs={{0,16},{16,32},{32,48},{48,64},{64,80},{80,96},{96,112},{112,128},... | collective-permute-start | bytes 98312 | tf_op jit(solution)/shard_map/ppermute | solution.py:18
  33.0 4.7 %collective-permute-start.5 = (bf16[128,128]{0,1:T(8,128)(2,1)S(1)}, bf16[128,128]{0,1:T(8,128)(2,1)S(1)}, u32[]{:S(2)}, u32[]{:S(2)}) collective-permute-start(bf16[128,128]{0,1:T(8,128)(2,1)S(1)} %collective-permute-done.4), channel_id=1, source_target_pairs={{16,0},{32,16},{48,32},{64,48},{80,64},{96,80},{112,96},{128,112},... | collective-permute-start | bytes 98312 | tf_op jit(solution)/shard_map/ppermute | solution.py:18
  37.6 4.6 %collective-permute-start.6 = (bf16[128,128]{0,1:T(8,128)(2,1)S(1)}, bf16[128,128]{0,1:T(8,128)(2,1)S(1)}, u32[]{:S(2)}, u32[]{:S(2)}) collective-permute-start(bf16[128,128]{0,1:T(8,128)(2,1)S(1)} %collective-permute-done.5), channel_id=1, source_target_pairs={{16,0},{32,16},{48,32},{64,48},{80,64},{96,80},{112,96},{128,112},... | collective-permute-start | bytes 98312 | tf_op jit(solution)/shard_map/ppermute | solution.py:18
  42.3 0.7 copy-start
Sparse Core Ops, SparseCore 0:
  43.1 60.6 all-gather.1
where the time goes:
time: 345 us; the launch traced here: 339 us
  matrix products  228 us (66%)
  waiting for transfers between devices  64 us (19%)
  starting transfers between devices  19.2 us (6%)
  between operations  16.6 us (5%)
  local copies, waits for them, and re-layouts  6.69 us (2%)
    dot_general x10, matrix products, split_product(): jnp.dot(series, lower, preferred_element_type=jnp.float32)  83.5 us
    dot_general x10, matrix products, split_product(): jnp.dot(series, upper, preferred_element_type=jnp.float32)  82.5 us
    all_gather x1, waiting for transfers between devices, per_device(): whole_window = lax.all_gather(window, 'pair', axis=1, tiled=True)  57.4 us
    dot_general x10, matrix products, split_einsum(): jnp.einsum('lk,sak->sla', table_upper, spec_lower, preferred_element_type...  19.3 us
    dot_general x10, matrix products, split_einsum(): jnp.einsum('lk,sak->sla', table_lower, spec_upper, preferred_element_type...  18.1 us
    dot_general x10, matrix products, split_einsum(): jnp.einsum('lk,sak->sla', table_upper, spec_upper, preferred_element_type...  17.7 us
    ppermute x5, starting transfers between devices, from_behind(): lax.ppermute(value, axis, [(source, source + steps) for source in range(f...  9.14 us
  transfers between devices with their start and end apart: 8, of which 3 were waited for; matrix products, arithmetic and copies ran while one was open for 1% of the time, Pallas kernels for 0%

commit v1 on v0

v1 whole, which is shorter than its diff:
```python
import math

import jax
import jax.numpy as jnp
import ml_dtypes
import numpy as np
from jax import lax
from jax.experimental import pallas as pl
from jax.experimental.pallas import tpu as pltpu
from jax.sharding import PartitionSpec as P

LAG = 200
REACH = 2
EPSILON = 1e-05
FREQ = 128
LAG_PAD = 512


def transform_tables(samples):
    length = -(-(samples + LAG) // (2 * FREQ)) * 2 * FREQ
    steps = length // 2 // FREQ
    theta = 2 * np.pi * (np.arange(length // 2) + 0.5) / length
    angle = np.outer(np.arange(samples), theta)
    cosine = np.cos(angle).reshape(samples, steps, FREQ)
    sine = np.sin(angle).reshape(samples, steps, FREQ)
    forward = np.concatenate([cosine, sine], 2).transpose(1, 0, 2)
    angle = np.outer(theta, np.arange(LAG_PAD) - LAG)
    weight = 2.0 / length / math.sqrt(samples)
    cosine = (np.cos(angle) * weight).reshape(steps, FREQ, LAG_PAD)
    sine = (np.sin(angle) * weight).reshape(steps, FREQ, LAG_PAD)
    backward = np.concatenate([cosine, sine], 1)
    return forward.astype(ml_dtypes.bfloat16), backward.astype(ml_dtypes.bfloat16)


def correlate_kernel(raw_ref, taps_ref, live_ref, forward_ref, backward_ref, out_ref, unit_ref):
    pieces, rows, width = raw_ref.shape
    half = rows // 2
    span = taps_ref.shape[1]
    taps = taps_ref[...].astype(jnp.bfloat16).astype(jnp.float32)
    total = jnp.sum(taps)
    band = pltpu.roll(
        jnp.broadcast_to(taps, (2 * width, span)), 0, 1, stride=1, stride_axis=0
    ).astype(jnp.bfloat16)
    outside = jnp.zeros((rows, width), jnp.bfloat16)
    for first in range(0, pieces, 2):
        parts = [
            raw_ref[p] if 0 <= p < pieces else outside for p in range(first - 1, first + 3)
        ]
        smoothed = lax.dot_general(
            jnp.abs(jnp.concatenate(parts, 1)),
            band,
            (((1,), (1,)), ((), ())),
            preferred_element_type=jnp.float32,
        )
        values = jnp.concatenate(parts[1:3], 1).astype(jnp.float32)
        unit_ref[:, first * width : (first + 2) * width] = (
            values / (smoothed / total + EPSILON)
        ).astype(jnp.bfloat16)
    result = jnp.zeros((half, LAG_PAD), jnp.float32)
    for step in range(forward_ref.shape[0]):
        spectra = jnp.dot(unit_ref[...], forward_ref[step], preferred_element_type=jnp.float32)
        own_cos, own_sin = spectra[:half, :FREQ], spectra[:half, FREQ:]
        far_cos, far_sin = spectra[half:, :FREQ], spectra[half:, FREQ:]
        product = jnp.concatenate(
            [own_cos * far_cos + own_sin * far_sin, own_cos * far_sin - own_sin * far_cos], 1
        ).astype(jnp.bfloat16)
        result = result + jnp.dot(
            product, backward_ref[step], preferred_element_type=jnp.float32
        )
    out_ref[...] = (result * live_ref[0]).T[: out_ref.shape[0]]


def correlate(raw, smooth_taps, live):
    pieces, rows, width = raw.shape
    forward, backward = transform_tables(pieces * width)
    lead = width - (smooth_taps.shape[0] - 1) // 2
    taps = jnp.pad(smooth_taps, (lead, 4 * width - lead - smooth_taps.shape[0]))[None]
    whole = pl.BlockSpec(memory_space=pltpu.VMEM)
    return pl.pallas_call(
        correlate_kernel,
        out_shape=jax.ShapeDtypeStruct((2 * LAG + 1, rows // 2), jnp.float32),
        in_specs=[whole, whole, pl.BlockSpec(memory_space=pltpu.SMEM), whole, whole],
        out_specs=whole,
        scratch_shapes=[pltpu.VMEM((rows, pieces * width), jnp.bfloat16)],
        compiler_params=pltpu.CompilerParams(vmem_limit_bytes=40 << 20),
    )(raw, taps, live, jnp.asarray(forward), jnp.asarray(backward))


def from_behind(value, axis, steps):
    count = lax.axis_size(axis)
    first, last = (max(0, -steps), min(count, count - steps))
    return lax.ppermute(value, axis, [(source, source + steps) for source in range(first, last)])


def per_device(raw_strain, smooth_taps, partner_block, chan_offset, pair_count):
    block_rows = raw_strain.shape[0]
    cable_place = lax.axis_index("cable")
    pair_place = lax.axis_index("pair")
    lower = [from_behind(raw_strain, "cable", d) for d in range(REACH, 0, -1)]
    upper = [from_behind(raw_strain, "cable", -d) for d in range(1, REACH + 2)]
    window = jnp.concatenate(lower + [raw_strain] + upper, 0)
    starts = (partner_block[0] - cable_place + REACH) * block_rows + chan_offset[0]
    picked = [
        jnp.concatenate(
            [raw_strain, lax.dynamic_slice_in_dim(window, starts[s], block_rows, 0)], 0
        )
        for s in range(starts.shape[0])
    ]
    records = lax.all_to_all(jnp.stack(picked, 0), "pair", 0, 0)
    live = (pair_place < pair_count[0]).astype(jnp.float32)
    return correlate(records, smooth_taps, live[None])[None, None]


def solution(mesh):
    in_specs = (P("cable", "pair"), P(), P("cable", None), P("cable", None), P("cable"))
    out_specs = P("cable", "pair", None, None)
    return jax.shard_map(
        per_device, mesh=mesh, in_specs=in_specs, out_specs=out_specs, check_vma=False
    )
```

time: 345 us -> 129 us (0.37)
  the two profiles are of different devices: /device:TPU:1 before, /device:TPU:43 now
where the time goes in v1:
time: 129 us; the launch traced here: 127 us
  starting transfers between devices  31.7 us (25%)
  between operations  30.7 us (24%)
  waiting for transfers between devices  26.6 us (21%)
  other arithmetic  22.9 us (18%)
  local copies, waits for them, and re-layouts  8.79 us (7%)
  Pallas kernels  6.71 us (5%)
    all_to_all x1, waiting for transfers between devices, per_device(): records = lax.all_to_all(jnp.stack(picked, 0), 'pair', 0, 0)  26.5 us
    unnamed x15, other arithmetic  20.8 us
    ppermute x5, starting transfers between devices, from_behind(): lax.ppermute(value, axis, [(source, source + steps) for source in range(f...  19.3 us
    all_to_all x1, starting transfers between devices, per_device(): records = lax.all_to_all(jnp.stack(picked, 0), 'pair', 0, 0)  12.4 us
    pallas_call x1, Pallas kernels, correlate(): pl.pallas_call(correlate_kernel, out_shape=jax.ShapeDtypeStruct((2 * LAG...  6.71 us
    unnamed x9, local copies, waits for them, and re-layouts  6.15 us
  transfers between devices with their start and end apart: 6, of which 1 were waited for; matrix products, arithmetic and copies ran while one was open for 2% of the time, Pallas kernels for 0%

profile of v1, /device:TPU:43, one launch (start us, length us, event | category | flops | bytes accessed | tf_op | source)
XLA Modules:
  0.0 127.3 jit_solution(10590651705573726094)
XLA Ops:
  0.0 3.7 %collective-permute-start = (bf16[128,128]{1,0:T(8,128)(2,1)}, bf16[128,128]{1,0:T(8,128)(2,1)S(1)}, u32[]{:S(2)}, u32[]{:S(2)}) collective-permute-start(bf16[128,128]{1,0:T(8,128)(2,1)} %param.7), channel_id=1, source_target_pairs={{0,32},{16,48},{32,64},{48,80},{64,96},{80,112},{96,128},{112,144}... | collective-permute-start | bytes 98312 | tf_op jit(solution)/shard_map/ppermute | solution.py:92
  3.8 1.9 %collective-permute-start.1 = (bf16[128,128]{1,0:T(8,128)(2,1)}, bf16[128,128]{1,0:T(8,128)(2,1)S(1)}, u32[]{:S(2)}, u32[]{:S(2)}) collective-permute-start(bf16[128,128]{1,0:T(8,128)(2,1)} %param.7), channel_id=1, source_target_pairs={{0,16},{16,32},{32,48},{48,64},{64,80},{80,96},{96,112},{112,128},... | collective-permute-start | bytes 98312 | tf_op jit(solution)/shard_map/ppermute | solution.py:92
  5.7 3.4 %collective-permute-start.2 = (bf16[128,128]{1,0:T(8,128)(2,1)}, bf16[128,128]{1,0:T(8,128)(2,1)S(1)}, u32[]{:S(2)}, u32[]{:S(2)}) collective-permute-start(bf16[128,128]{1,0:T(8,128)(2,1)} %param.7), channel_id=1, source_target_pairs={{16,0},{32,16},{48,32},{64,48},{80,64},{96,80},{112,96},{128,112},... | collective-permute-start | bytes 98312 | tf_op jit(solution)/shard_map/ppermute | solution.py:92
  9.1 4.3 %collective-permute-start.3 = (bf16[128,128]{1,0:T(8,128)(2,1)}, bf16[128,128]{1,0:T(8,128)(2,1)S(1)}, u32[]{:S(2)}, u32[]{:S(2)}) collective-permute-start(bf16[128,128]{1,0:T(8,128)(2,1)} %param.7), channel_id=1, source_target_pairs={{32,0},{48,16},{64,32},{80,48},{96,64},{112,80},{128,96},{144,112}... | collective-permute-start | bytes 98312 | tf_op jit(solution)/shard_map/ppermute | solution.py:92
  13.4 6.0 %collective-permute-start.4 = (bf16[128,128]{1,0:T(8,128)(2,1)}, bf16[128,128]{1,0:T(8,128)(2,1)S(1)}, u32[]{:S(2)}, u32[]{:S(2)}) collective-permute-start(bf16[128,128]{1,0:T(8,128)(2,1)} %param.7), channel_id=1, source_target_pairs={{48,0},{64,16},{80,32},{96,48},{112,64},{128,80},{144,96},{160,112... | collective-permute-start | bytes 98312 | tf_op jit(solution)/shard_map/ppermute | solution.py:92
  19.3 0.7 multiply_add_fusion
  20.0 0.7 fusion.32
  50.6 0.0 collective-permute-done
  50.6 0.0 collective-permute-done.1
  50.7 0.8 constant_dynamic-update-slice_fusion.3
  51.4 0.0 collective-permute-done.2
  51.4 0.0 collective-permute-done.3
  51.5 0.0 collective-permute-done.4
  51.5 0.3 constant_dynamic-slice_fusion
  51.8 1.4 %fusion.1 = bf16[16,256,128]{2,1,0:T(8,128)(2,1)} fusion(bf16[128,128]{1,0:T(8,128)(2,1)} %param.7, bf16[128,128]{1,0:T(8,128)(2,1)S(1)} %get-tuple-element.20), kind=kLoop, calls=%fused_computation.17 | loop fusion | flops 131071 | bytes 131072
  53.2 1.4 %fusion.3 = bf16[16,256,128]{2,1,0:T(8,128)(2,1)} fusion(bf16[16,256,128]{2,1,0:T(8,128)(2,1)} %fusion.1, bf16[128,128]{1,0:T(8,128)(2,1)} %param.7, bf16[128,128]{1,0:T(8,128)(2,1)S(1)} %get-tuple-element.19), kind=kLoop, calls=%fused_computation.19 | loop fusion | flops 131072 | bytes 131072
  54.6 1.4 %fusion.5 = bf16[16,256,128]{2,1,0:T(8,128)(2,1)} fusion(bf16[16,256,128]{2,1,0:T(8,128)(2,1)} %fusion.3, bf16[128,128]{1,0:T(8,128)(2,1)} %param.7, bf16[128,128]{1,0:T(8,128)(2,1)S(1)} %get-tuple-element.18), kind=kLoop, calls=%fused_computation.21 | loop fusion | flops 131072 | bytes 131072
  56.0 1.4 %fusion.7 = bf16[16,256,128]{2,1,0:T(8,128)(2,1)} fusion(bf16[16,256,128]{2,1,0:T(8,128)(2,1)} %fusion.5, bf16[128,128]{1,0:T(8,128)(2,1)} %param.7, bf16[128,128]{1,0:T(8,128)(2,1)S(1)} %get-tuple-element.17), kind=kLoop, calls=%fused_computation.23 | loop fusion | flops 131072 | bytes 131072
  57.3 1.4 %fusion.9 = bf16[16,256,128]{2,1,0:T(8,128)(2,1)} fusion(bf16[16,256,128]{2,1,0:T(8,128)(2,1)} %fusion.7, bf16[128,128]{1,0:T(8,128)(2,1)} %param.7, bf16[128,128]{1,0:T(8,128)(2,1)S(1)} %get-tuple-element.16), kind=kLoop, calls=%fused_computation.25 | loop fusion | flops 131072 | bytes 131072
  58.7 1.4 %fusion.11 = bf16[16,256,128]{2,1,0:T(8,128)(2,1)} fusion(bf16[16,256,128]{2,1,0:T(8,128)(2,1)} %fusion.9, bf16[128,128]{1,0:T(8,128)(2,1)} %param.7, bf16[128,128]{1,0:T(8,128)(2,1)S(1)} %get-tuple-element.15), kind=kLoop, calls=%fused_computation.27 | loop fusion | flops 131072 | bytes 131072
  60.1 1.4 %fusion.13 = bf16[16,256,128]{2,1,0:T(8,128)(2,1)} fusion(bf16[16,256,128]{2,1,0:T(8,128)(2,1)} %fusion.11, bf16[128,128]{1,0:T(8,128)(2,1)} %param.7, bf16[128,128]{1,0:T(8,128)(2,1)S(1)} %get-tuple-element.14), kind=kLoop, calls=%fused_computation.29 | loop fusion | flops 131072 | bytes 131072
  61.5 1.4 %fusion.15 = bf16[16,256,128]{2,1,0:T(8,128)(2,1)} fusion(bf16[16,256,128]{2,1,0:T(8,128)(2,1)} %fusion.13, bf16[128,128]{1,0:T(8,128)(2,1)} %param.7, bf16[128,128]{1,0:T(8,128)(2,1)S(1)} %get-tuple-element.13), kind=kLoop, calls=%fused_computation.31 | loop fusion | flops 131072 | bytes 131072
  62.9 1.4 %fusion.17 = bf16[16,256,128]{2,1,0:T(8,128)(2,1)} fusion(bf16[16,256,128]{2,1,0:T(8,128)(2,1)} %fusion.15, bf16[128,128]{1,0:T(8,128)(2,1)} %param.7, bf16[128,128]{1,0:T(8,128)(2,1)S(1)} %get-tuple-element.12), kind=kLoop, calls=%fused_computation.33 | loop fusion | flops 131072 | bytes 131072
  64.3 1.4 %fusion.19 = bf16[16,256,128]{2,1,0:T(8,128)(2,1)} fusion(bf16[16,256,128]{2,1,0:T(8,128)(2,1)} %fusion.17, bf16[128,128]{1,0:T(8,128)(2,1)} %param.7, bf16[128,128]{1,0:T(8,128)(2,1)S(1)} %get-tuple-element.11), kind=kLoop, calls=%fused_computation.35 | loop fusion | flops 131072 | bytes 131072
  65.7 1.4 %fusion.21 = bf16[16,256,128]{2,1,0:T(8,128)(2,1)} fusion(bf16[16,256,128]{2,1,0:T(8,128)(2,1)} %fusion.19, bf16[128,128]{1,0:T(8,128)(2,1)} %param.7, bf16[128,128]{1,0:T(8,128)(2,1)S(1)} %get-tuple-element.10), kind=kLoop, calls=%fused_computation.37 | loop fusion | flops 131072 | bytes 131072
  67.1 1.4 %fusion.23 = bf16[16,256,128]{2,1,0:T(8,128)(2,1)} fusion(bf16[16,256,128]{2,1,0:T(8,128)(2,1)} %fusion.21, bf16[128,128]{1,0:T(8,128)(2,1)} %param.7, bf16[128,128]{1,0:T(8,128)(2,1)S(1)} %get-tuple-element.9), kind=kLoop, calls=%fused_computation.39 | loop fusion | flops 131072 | bytes 131072
  68.4 1.4 %fusion.25 = bf16[16,256,128]{2,1,0:T(8,128)(2,1)} fusion(bf16[16,256,128]{2,1,0:T(8,128)(2,1)} %fusion.23, bf16[128,128]{1,0:T(8,128)(2,1)} %param.7, bf16[128,128]{1,0:T(8,128)(2,1)S(1)} %get-tuple-element.8), kind=kLoop, calls=%fused_computation.41 | loop fusion | flops 131072 | bytes 131072
  69.8 1.4 %fusion.27 = bf16[16,256,128]{2,1,0:T(8,128)(2,1)} fusion(bf16[16,256,128]{2,1,0:T(8,128)(2,1)} %fusion.25, bf16[128,128]{1,0:T(8,128)(2,1)} %param.7, bf16[128,128]{1,0:T(8,128)(2,1)S(1)} %get-tuple-element.7), kind=kLoop, calls=%fused_computation.43 | loop fusion | flops 131072 | bytes 131072
  71.2 1.4 %fusion.29 = bf16[16,256,128]{2,1,0:T(8,128)(2,1)} fusion(bf16[16,256,128]{2,1,0:T(8,128)(2,1)} %fusion.27, bf16[128,128]{1,0:T(8,128)(2,1)} %param.7, bf16[128,128]{1,0:T(8,128)(2,1)S(1)} %get-tuple-element.6), kind=kLoop, calls=%fused_computation.45 | loop fusion | flops 131072 | bytes 131072
  72.6 1.4 %fusion.31 = bf16[16,256,128]{2,1,0:T(8,128)(2,1)} fusion(bf16[16,256,128]{2,1,0:T(8,128)(2,1)} %fusion.29, bf16[128,128]{1,0:T(8,128)(2,1)} %param.7, bf16[128,128]{1,0:T(8,128)(2,1)S(1)} %get-tuple-element.5), kind=kLoop, calls=%fused_computation.47 | loop fusion | flops 131072 | bytes 131072 | tf_op jit(solution)/shard_map/stack | solution.py:109
  74.0 12.4 %all-to-all-start = ((bf16[16,256,128]{2,1,0:T(8,128)(2,1)}), bf16[16,256,128]{2,1,0:T(8,128)(2,1)S(1)}, u32[]{:S(2)}, u32[]{:S(2)}) async-start(bf16[16,256,128]{2,1,0:T(8,128)(2,1)} %fusion.31), calls=%async_computation | async-start | bytes 2097152 | tf_op jit(solution)/shard_map/all_to_all | solution.py:109
  87.0 0.7 pad.4
  87.8 26.5 %all-to-all-done.raw_ref = bf16[16,256,128]{2,1,0:T(8,128)(2,1)S(1)} async-done(((bf16[16,256,128]{2,1,0:T(8,128)(2,1)}), bf16[16,256,128]{2,1,0:T(8,128)(2,1)S(1)}, u32[]{:S(2)}, u32[]{:S(2)}) %all-to-all-start) | async-done | bytes 1048608 | tf_op jit(solution)/shard_map/all_to_all | solution.py:109
  114.3 0.0 copy-start
  114.3 3.7 %copy-done = bf16[9,2048,256]{2,1,0:T(8,128)(2,1)S(1)} copy-done((bf16[9,2048,256]{2,1,0:T(8,128)(2,1)S(1)}, bf16[9,2048,256]{2,1,0:T(8,128)(2,1)}, u32[]{:S(2)}) %copy-start) | copy-done | bytes 9437208
  118.0 0.0 copy-start.1
  118.0 1.7 %copy-done.1 = bf16[9,256,512]{2,1,0:T(8,128)(2,1)S(1)} copy-done((bf16[9,256,512]{2,1,0:T(8,128)(2,1)S(1)}, bf16[9,256,512]{2,1,0:T(8,128)(2,1)}, u32[]{:S(2)}) %copy-start.1) | copy-done | bytes 2359320
  119.7 6.7 %shard_map.73 = f32[401,128]{1,0:T(8,128)S(1)} custom-call(bf16[16,256,128]{2,1,0:T(8,128)(2,1)S(1)} %all-to-all-done.raw_ref, f32[1,512]{1,0:T(1,128)S(1)} %bitcast.86, f32[1]{0:T(128)} %bitcast.34.live_ref, bf16[9,2048,256]{2,1,0:T(8,128)(2,1)S(1)} %copy-done, bf16[9,256,512]{2,1,0:T(8,128)(2,1)S(1)} %copy-done.1), custom_call_target="tpu_custom_call" | custom-call | tf_op jit(solution)/shard_map/pallas_call | solution.py:79
  126.4 0.9 copy.8
  (5 shorter events, 0.0 us)
Async XLA Ops:
  0.0 50.6 %collective-permute-start = (bf16[128,128]{1,0:T(8,128)(2,1)}, bf16[128,128]{1,0:T(8,128)(2,1)S(1)}, u32[]{:S(2)}, u32[]{:S(2)}) collective-permute-start(bf16[128,128]{1,0:T(8,128)(2,1)} %param.7), channel_id=1, source_target_pairs={{0,32},{16,48},{32,64},{48,80},{64,96},{80,112},{96,128},{112,144}... | collective-permute-start | bytes 98312 | tf_op jit(solution)/shard_map/ppermute | solution.py:92
  3.8 46.9 %collective-permute-start.1 = (bf16[128,128]{1,0:T(8,128)(2,1)}, bf16[128,128]{1,0:T(8,128)(2,1)S(1)}, u32[]{:S(2)}, u32[]{:S(2)}) collective-permute-start(bf16[128,128]{1,0:T(8,128)(2,1)} %param.7), channel_id=1, source_target_pairs={{0,16},{16,32},{32,48},{48,64},{64,80},{80,96},{96,112},{112,128},... | collective-permute-start | bytes 98312 | tf_op jit(solution)/shard_map/ppermute | solution.py:92
  5.7 45.8 %collective-permute-start.2 = (bf16[128,128]{1,0:T(8,128)(2,1)}, bf16[128,128]{1,0:T(8,128)(2,1)S(1)}, u32[]{:S(2)}, u32[]{:S(2)}) collective-permute-start(bf16[128,128]{1,0:T(8,128)(2,1)} %param.7), channel_id=1, source_target_pairs={{16,0},{32,16},{48,32},{64,48},{80,64},{96,80},{112,96},{128,112},... | collective-permute-start | bytes 98312 | tf_op jit(solution)/shard_map/ppermute | solution.py:92
  9.1 42.4 %collective-permute-start.3 = (bf16[128,128]{1,0:T(8,128)(2,1)}, bf16[128,128]{1,0:T(8,128)(2,1)S(1)}, u32[]{:S(2)}, u32[]{:S(2)}) collective-permute-start(bf16[128,128]{1,0:T(8,128)(2,1)} %param.7), channel_id=1, source_target_pairs={{32,0},{48,16},{64,32},{80,48},{96,64},{112,80},{128,96},{144,112}... | collective-permute-start | bytes 98312 | tf_op jit(solution)/shard_map/ppermute | solution.py:92
  13.4 38.1 %collective-permute-start.4 = (bf16[128,128]{1,0:T(8,128)(2,1)}, bf16[128,128]{1,0:T(8,128)(2,1)S(1)}, u32[]{:S(2)}, u32[]{:S(2)}) collective-permute-start(bf16[128,128]{1,0:T(8,128)(2,1)} %param.7), channel_id=1, source_target_pairs={{48,0},{64,16},{80,32},{96,48},{112,64},{128,80},{144,96},{160,112... | collective-permute-start | bytes 98312 | tf_op jit(solution)/shard_map/ppermute | solution.py:92
  74.0 40.3 %all-to-all-start = ((bf16[16,256,128]{2,1,0:T(8,128)(2,1)}), bf16[16,256,128]{2,1,0:T(8,128)(2,1)S(1)}, u32[]{:S(2)}, u32[]{:S(2)}) async-start(bf16[16,256,128]{2,1,0:T(8,128)(2,1)} %fusion.31), calls=%async_computation | async-start | bytes 2097152 | tf_op jit(solution)/shard_map/all_to_all | solution.py:109
  114.3 3.7 %copy-start = (bf16[9,2048,256]{2,1,0:T(8,128)(2,1)S(1)}, bf16[9,2048,256]{2,1,0:T(8,128)(2,1)}, u32[]{:S(2)}) copy-start(bf16[9,2048,256]{2,1,0:T(8,128)(2,1)} %constant.23.clone.forward_ref) | copy-start | bytes 28311556
  118.0 1.7 %copy-start.1 = (bf16[9,256,512]{2,1,0:T(8,128)(2,1)S(1)}, bf16[9,256,512]{2,1,0:T(8,128)(2,1)}, u32[]{:S(2)}) copy-start(bf16[9,256,512]{2,1,0:T(8,128)(2,1)} %constant.24.clone.backward_ref) | copy-start | bytes 7077892

commit v2 on v1

v2 whole, which is shorter than its diff:
```python
import math

import jax
import jax.numpy as jnp
import ml_dtypes
import numpy as np
from jax import lax
from jax.experimental import pallas as pl
from jax.experimental.pallas import tpu as pltpu
from jax.sharding import PartitionSpec as P

LAG = 200
REACH = 2
EPSILON = 1e-05
WIDE = 256
LAG_PAD = 512


def transform_tables(samples):
    length = -(-(samples + LAG) // WIDE) * WIDE
    theta = 2 * np.pi * (np.arange(length // 2) + 0.5) / length
    forward = np.outer(np.arange(samples // 2) + 0.5, theta)
    backward = np.outer(theta, np.arange(LAG_PAD) - LAG)
    weight = 2.0 / length / math.sqrt(samples)
    tables = (
        np.cos(forward),
        np.sin(forward),
        np.cos(backward) * weight,
        np.sin(backward) * weight,
    )
    return [jnp.asarray(table.astype(ml_dtypes.bfloat16)) for table in tables]


def correlate_kernel(
    raw_ref,
    taps_hbm,
    cos_hbm,
    sin_hbm,
    back_cos_hbm,
    back_sin_hbm,
    out_hbm,
    taps_ref,
    cos_ref,
    sin_ref,
    back_cos_ref,
    back_sin_ref,
    row_ref,
    unit_ref,
    even_ref,
    odd_ref,
    real_ref,
    imag_ref,
    out_ref,
    copied,
):
    pieces, rows, width = raw_ref.shape
    half = rows // 2
    frequencies = cos_ref.shape[1]
    starts = range(0, frequencies, WIDE)
    taps_copy = pltpu.make_async_copy(taps_hbm, taps_ref, copied.at[0])
    taps_copy.start()
    copies = []
    for start in starts:
        part = pl.ds(start, min(WIDE, frequencies - start))
        for source, target in ((cos_hbm, cos_ref), (sin_hbm, sin_ref)):
            copies.append(
                pltpu.make_async_copy(
                    source.at[:, part], target.at[:, part], copied.at[1 + len(copies)]
                )
            )
    for source, target in ((back_cos_hbm, back_cos_ref), (back_sin_hbm, back_sin_ref)):
        copies.append(pltpu.make_async_copy(source, target, copied.at[1 + len(copies)]))
    for copy in copies:
        copy.start()

    row_ref[...] = jnp.zeros_like(row_ref)
    lead = width - (taps_ref.shape[1] - 1) // 2
    taps_copy.wait()
    row_ref[:, lead : lead + taps_ref.shape[1]] = taps_ref[...]
    taps = row_ref[...].astype(jnp.bfloat16).astype(jnp.float32)
    scale = 1.0 / jnp.sum(taps)
    band = pltpu.roll(
        jnp.broadcast_to(taps, (WIDE, row_ref.shape[1])), 0, 1, stride=1, stride_axis=0
    ).astype(jnp.bfloat16)
    outside = jnp.zeros((rows, width), jnp.bfloat16)
    for first in range(0, pieces, 2):
        parts = [
            raw_ref[p] if 0 <= p < pieces else outside for p in range(first - 1, first + 3)
        ]
        smoothed = lax.dot_general(
            jnp.abs(jnp.concatenate(parts, 1)),
            band,
            (((1,), (1,)), ((), ())),
            preferred_element_type=jnp.float32,
        )
        values = jnp.concatenate(parts[1:3], 1).astype(jnp.float32)
        unit_ref[:, first * width : first * width + WIDE] = (
            values / (smoothed * scale + EPSILON)
        ).astype(jnp.bfloat16)

    mirror = (
        lax.broadcasted_iota(jnp.int32, (WIDE, WIDE), 0)
        + lax.broadcasted_iota(jnp.int32, (WIDE, WIDE), 1)
        == WIDE - 1
    ).astype(jnp.bfloat16)
    middle = even_ref.shape[1]
    for start in range(0, middle, WIDE):
        mirrored = jnp.dot(
            unit_ref[:, middle - start - WIDE : middle - start],
            mirror,
            preferred_element_type=jnp.float32,
        )
        later = unit_ref[:, middle + start : middle + start + WIDE].astype(jnp.float32)
        even_ref[:, start : start + WIDE] = (later + mirrored).astype(jnp.bfloat16)
        odd_ref[:, start : start + WIDE] = (later - mirrored).astype(jnp.bfloat16)

    for step, start in enumerate(starts):
        stop = min(start + WIDE, frequencies)
        copies[2 * step].wait()
        copies[2 * step + 1].wait()
        cosine = jnp.dot(
            even_ref[...], cos_ref[:, start:stop], preferred_element_type=jnp.float32
        )
        sine = jnp.dot(odd_ref[...], sin_ref[:, start:stop], preferred_element_type=jnp.float32)
        own_cos, far_cos = cosine[:half], cosine[half:]
        own_sin, far_sin = sine[:half], sine[half:]
        real_ref[:, start:stop] = (own_cos * far_cos + own_sin * far_sin).astype(jnp.bfloat16)
        imag_ref[:, start:stop] = (own_cos * far_sin - own_sin * far_cos).astype(jnp.bfloat16)
    copies[-2].wait()
    copies[-1].wait()
    result = jnp.dot(
        real_ref[...], back_cos_ref[...], preferred_element_type=jnp.float32
    ) + jnp.dot(imag_ref[...], back_sin_ref[...], preferred_element_type=jnp.float32)
    out_ref[...] = result.T[: out_ref.shape[0]]
    written = pltpu.make_async_copy(out_ref, out_hbm.at[:, 0], copied.at[0])
    written.start()
    written.wait()


def correlate(raw, smooth_taps):
    pieces, rows, width = raw.shape
    samples = pieces * width
    tables = transform_tables(samples)
    vmem = pl.BlockSpec(memory_space=pltpu.VMEM)
    hbm = pl.BlockSpec(memory_space=pltpu.HBM)
    frequencies = tables[0].shape[1]
    copies = 2 * -(-frequencies // WIDE) + 2
    return pl.pallas_call(
        correlate_kernel,
        out_shape=jax.ShapeDtypeStruct((2 * LAG + 1, 1, rows // 2), jnp.float32),
        in_specs=[vmem] + [hbm] * 5,
        out_specs=hbm,
        scratch_shapes=[pltpu.VMEM((1, smooth_taps.shape[0]), jnp.float32)]
        + [pltpu.VMEM(table.shape, jnp.bfloat16) for table in tables]
        + [
            pltpu.VMEM((1, 2 * WIDE), jnp.float32),
            pltpu.VMEM((rows, samples), jnp.bfloat16),
            pltpu.VMEM((rows, samples // 2), jnp.bfloat16),
            pltpu.VMEM((rows, samples // 2), jnp.bfloat16),
            pltpu.VMEM((rows // 2, frequencies), jnp.bfloat16),
            pltpu.VMEM((rows // 2, frequencies), jnp.bfloat16),
            pltpu.VMEM((2 * LAG + 1, rows // 2), jnp.float32),
            pltpu.SemaphoreType.DMA((1 + copies,)),
        ],
        compiler_params=pltpu.CompilerParams(vmem_limit_bytes=56 << 20),
    )(raw, smooth_taps[None], *tables)


def pick_kernel(start_ref, window_ref, out_ref, wide_ref):
    slots, rows = out_ref.shape[0], out_ref.shape[1] // 2
    window_rows = window_ref.shape[0]
    wide_ref[:window_rows] = window_ref[...].astype(jnp.float32)
    wide_ref[window_rows:] = jnp.zeros_like(wide_ref[window_rows:])
    own = window_ref[REACH * rows : (REACH + 1) * rows]
    for slot in range(slots):
        out_ref[slot, :rows] = own
        out_ref[slot, rows:] = wide_ref[pl.ds(start_ref[slot], rows)].astype(jnp.bfloat16)


def pick(starts, window, rows):
    window_rows, width = window.shape
    vmem = pl.BlockSpec(memory_space=pltpu.VMEM)
    smem = pl.BlockSpec(memory_space=pltpu.SMEM)
    return pl.pallas_call(
        pick_kernel,
        out_shape=jax.ShapeDtypeStruct((starts.shape[0], 2 * rows, width), jnp.bfloat16),
        in_specs=[smem, vmem],
        out_specs=vmem,
        scratch_shapes=[pltpu.VMEM((window_rows + rows, width), jnp.float32)],
        compiler_params=pltpu.CompilerParams(vmem_limit_bytes=8 << 20),
    )(starts, window)


def from_behind(value, axis, steps):
    count = lax.axis_size(axis)
    first, last = (max(0, -steps), min(count, count - steps))
    return lax.ppermute(value, axis, [(source, source + steps) for source in range(first, last)])


def per_device(raw_strain, smooth_taps, partner_block, chan_offset, pair_count):
    rows = raw_strain.shape[0]
    first_block = lax.axis_index("cable") - REACH
    lower = [from_behind(raw_strain, "cable", d) for d in range(REACH, 0, -1)]
    upper = [from_behind(raw_strain, "cable", -d) for d in range(1, REACH + 2)]
    window = jnp.concatenate(lower + [raw_strain] + upper, 0)
    starts = (partner_block[0] - first_block) * rows + chan_offset[0]
    live = jnp.arange(starts.shape[0], dtype=jnp.int32) < pair_count
    starts = jnp.where(live, starts, window.shape[0])
    window, starts = lax.optimization_barrier((window, starts))
    records = lax.all_to_all(pick(starts, window, rows), "pair", 0, 0)
    return correlate(records, smooth_taps).reshape(1, 1, 2 * LAG + 1, rows)


def solution(mesh):
    in_specs = (P("cable", "pair"), P(), P("cable", None), P("cable", None), P("cable"))
    out_specs = P("cable", "pair", None, None)
    return jax.shard_map(
        per_device, mesh=mesh, in_specs=in_specs, out_specs=out_specs, check_vma=False
    )
```

time: 129 us -> 71.8 us (0.56)
  the two profiles are of different devices: /device:TPU:43 before, /device:TPU:27 now
where the time goes in v2:
time: 71.8 us; the launch traced here: 71.5 us
  blocking collectives  41.7 us (58%)
  starting transfers between devices  17.3 us (24%)
  Pallas kernels  7.31 us (10%)
  waiting for transfers between devices  2.89 us (4%)
  local copies, waits for them, and re-layouts  0.81 us (1%)
  between operations  0.73 us (1%)
    all_to_all x1, blocking collectives, per_device(): records = lax.all_to_all(pick(starts, window, rows), 'pair', 0, 0)  41.7 us
    ppermute x5, starting transfers between devices, from_behind(): lax.ppermute(value, axis, [(source, source + steps) for source in range(f...  17.3 us
    pallas_call x1, Pallas kernels, correlate(): pl.pallas_call(correlate_kernel, out_shape=jax.ShapeDtypeStruct((2 * LAG...  6.62 us
    ppermute x5, waiting for transfers between devices, from_behind(): lax.ppermute(value, axis, [(source, source + steps) for source in range(f...  2.89 us
  transfers between devices with their start and end apart: 5, of which 1 were waited for; matrix products, arithmetic and copies ran while one was open for 2% of the time, Pallas kernels for 0%

profile of v2, /device:TPU:27, one launch (start us, length us, event | category | flops | bytes accessed | tf_op | source)
XLA Modules:
  0.0 71.5 jit_solution(5360569505117181198)
XLA Ops:
  0.0 3.6 %collective-permute-start.3 = (bf16[128,128]{1,0:T(8,128)(2,1)}, bf16[128,128]{1,0:T(8,128)(2,1)S(1)}, u32[]{:S(2)}, u32[]{:S(2)}) collective-permute-start(bf16[128,128]{1,0:T(8,128)(2,1)} %param.9), channel_id=1, source_target_pairs={{32,0},{48,16},{64,32},{80,48},{96,64},{112,80},{128,96},{144,112}... | collective-permute-start | bytes 98312 | tf_op jit(solution)/shard_map/ppermute | solution.py:197
  3.6 3.1 %collective-permute-start.2 = (bf16[128,128]{1,0:T(8,128)(2,1)}, bf16[128,128]{1,0:T(8,128)(2,1)S(1)}, u32[]{:S(2)}, u32[]{:S(2)}) collective-permute-start(bf16[128,128]{1,0:T(8,128)(2,1)} %param.9), channel_id=1, source_target_pairs={{16,0},{32,16},{48,32},{64,48},{80,64},{96,80},{112,96},{128,112},... | collective-permute-start | bytes 98312 | tf_op jit(solution)/shard_map/ppermute | solution.py:197
  6.7 2.2 %collective-permute-start.1 = (bf16[128,128]{1,0:T(8,128)(2,1)}, bf16[128,128]{1,0:T(8,128)(2,1)S(1)}, u32[]{:S(2)}, u32[]{:S(2)}) collective-permute-start(bf16[128,128]{1,0:T(8,128)(2,1)} %param.9), channel_id=1, source_target_pairs={{0,16},{16,32},{32,48},{48,64},{64,80},{80,96},{96,112},{112,128},... | collective-permute-start | bytes 98312 | tf_op jit(solution)/shard_map/ppermute | solution.py:197
  8.9 6.5 %collective-permute-start = (bf16[128,128]{1,0:T(8,128)(2,1)}, bf16[128,128]{1,0:T(8,128)(2,1)S(1)}, u32[]{:S(2)}, u32[]{:S(2)}) collective-permute-start(bf16[128,128]{1,0:T(8,128)(2,1)} %param.9), channel_id=1, source_target_pairs={{0,32},{16,48},{32,64},{48,80},{64,96},{80,112},{96,128},{112,144}... | collective-permute-start | bytes 98312 | tf_op jit(solution)/shard_map/ppermute | solution.py:197
  15.4 1.9 %collective-permute-start.4 = (bf16[128,128]{1,0:T(8,128)(2,1)}, bf16[128,128]{1,0:T(8,128)(2,1)S(1)}, u32[]{:S(2)}, u32[]{:S(2)}) collective-permute-start(bf16[128,128]{1,0:T(8,128)(2,1)} %param.9), channel_id=1, source_target_pairs={{48,0},{64,16},{80,32},{96,48},{112,64},{128,80},{144,96},{160,112... | collective-permute-start | bytes 98312 | tf_op jit(solution)/shard_map/ppermute | solution.py:197
  18.0 0.7 compare_select_fusion.start_ref
  18.7 0.0 collective-permute-done
  18.7 0.0 collective-permute-done.1
  18.7 0.8 %constant_dynamic-update-slice_fusion.3 = bf16[768,128]{1,0:T(8,128)(2,1)S(1)} fusion(bf16[768,128]{1,0:T(8,128)(2,1)S(1)} %constant_dynamic-update-slice_fusion.4, bf16[128,128]{1,0:T(8,128)(2,1)} %param.9), kind=kLoop, calls=%fused_computation.3 | loop fusion | bytes 65536
  19.5 0.0 collective-permute-done.2
  19.5 0.0 collective-permute-done.3
  19.5 2.9 %collective-permute-done.4 = bf16[128,128]{1,0:T(8,128)(2,1)S(1)} collective-permute-done((bf16[128,128]{1,0:T(8,128)(2,1)}, bf16[128,128]{1,0:T(8,128)(2,1)S(1)}, u32[]{:S(2)}, u32[]{:S(2)}) %collective-permute-start.4) | collective-permute-done | bytes 32800 | tf_op jit(solution)/shard_map/ppermute | solution.py:197
  22.4 0.7 shard_map.91
  23.1 41.7 %all_to_all.5.raw_ref = bf16[16,256,128]{2,1,0:T(8,128)(2,1)} all-to-all(bf16[16,256,128]{2,1,0:T(8,128)(2,1)S(1)} %shard_map.91), channel_id=1, replica_groups=mesh['cable'=32,'pair'=16] {'pair'}, dimensions={0} | all-to-all | bytes 2097152 | tf_op jit(solution)/shard_map/all_to_all | solution.py:210
  64.8 6.6 %shard_map.92 = f32[401,1,128]{2,1,0:T(1,128)} custom-call(bf16[16,256,128]{2,1,0:T(8,128)(2,1)} %all_to_all.5.raw_ref, f32[1,101]{1,0:T(1,128)} %bitcast.8, bf16[1024,1152]{1,0:T(8,128)(2,1)} %constant.21.clone.cos_hbm, bf16[1024,1152]{1,0:T(8,128)(2,1)} %constant.22.clone.sin_hbm, bf16[1152,512]{1,0:T(8,128)(2,1)} %constant.23.clone.back_cos_hbm, ...), custom_call_target="tpu_custom_call" | custom-call | tf_op jit(solution)/shard_map/pallas_call | solution.py:148
  (5 shorter events, 0.0 us)
Async XLA Ops:
  0.0 19.5 %collective-permute-start.3 = (bf16[128,128]{1,0:T(8,128)(2,1)}, bf16[128,128]{1,0:T(8,128)(2,1)S(1)}, u32[]{:S(2)}, u32[]{:S(2)}) collective-permute-start(bf16[128,128]{1,0:T(8,128)(2,1)} %param.9), channel_id=1, source_target_pairs={{32,0},{48,16},{64,32},{80,48},{96,64},{112,80},{128,96},{144,112}... | collective-permute-start | bytes 98312 | tf_op jit(solution)/shard_map/ppermute | solution.py:197
  3.6 15.8 %collective-permute-start.2 = (bf16[128,128]{1,0:T(8,128)(2,1)}, bf16[128,128]{1,0:T(8,128)(2,1)S(1)}, u32[]{:S(2)}, u32[]{:S(2)}) collective-permute-start(bf16[128,128]{1,0:T(8,128)(2,1)} %param.9), channel_id=1, source_target_pairs={{16,0},{32,16},{48,32},{64,48},{80,64},{96,80},{112,96},{128,112},... | collective-permute-start | bytes 98312 | tf_op jit(solution)/shard_map/ppermute | solution.py:197
  6.7 12.0 %collective-permute-start.1 = (bf16[128,128]{1,0:T(8,128)(2,1)}, bf16[128,128]{1,0:T(8,128)(2,1)S(1)}, u32[]{:S(2)}, u32[]{:S(2)}) collective-permute-start(bf16[128,128]{1,0:T(8,128)(2,1)} %param.9), channel_id=1, source_target_pairs={{0,16},{16,32},{32,48},{48,64},{64,80},{80,96},{96,112},{112,128},... | collective-permute-start | bytes 98312 | tf_op jit(solution)/shard_map/ppermute | solution.py:197
  8.9 9.7 %collective-permute-start = (bf16[128,128]{1,0:T(8,128)(2,1)}, bf16[128,128]{1,0:T(8,128)(2,1)S(1)}, u32[]{:S(2)}, u32[]{:S(2)}) collective-permute-start(bf16[128,128]{1,0:T(8,128)(2,1)} %param.9), channel_id=1, source_target_pairs={{0,32},{16,48},{32,64},{48,80},{64,96},{80,112},{96,128},{112,144}... | collective-permute-start | bytes 98312 | tf_op jit(solution)/shard_map/ppermute | solution.py:197
  15.4 7.0 %collective-permute-start.4 = (bf16[128,128]{1,0:T(8,128)(2,1)}, bf16[128,128]{1,0:T(8,128)(2,1)S(1)}, u32[]{:S(2)}, u32[]{:S(2)}) collective-permute-start(bf16[128,128]{1,0:T(8,128)(2,1)} %param.9), channel_id=1, source_target_pairs={{48,0},{64,16},{80,32},{96,48},{112,64},{128,80},{144,96},{160,112... | collective-permute-start | bytes 98312 | tf_op jit(solution)/shard_map/ppermute | solution.py:197

commit v3 on v1

v3 whole, which is shorter than its diff:
```python
import math

import jax
import jax.numpy as jnp
import ml_dtypes
import numpy as np
from jax import lax
from jax.experimental import pallas as pl
from jax.experimental.pallas import tpu as pltpu
from jax.sharding import PartitionSpec as P

LAG = 200
REACH = 2
EPSILON = 1e-05
WIDE = 256
LAG_PAD = 512
LANES = 128
F32 = jnp.float32
BF16 = jnp.bfloat16


def transform_tables(samples):
    length = -(-(samples + LAG) // WIDE) * WIDE
    theta = 2 * np.pi * (np.arange(length // 2) + 0.5) / length
    forward = np.outer(np.arange(samples // 2) + 0.5, theta)
    backward = np.outer(theta, np.arange(LAG_PAD) - LAG)
    weight = 2.0 / length / math.sqrt(samples)
    tables = (
        np.cos(forward),
        np.sin(forward),
        np.cos(backward) * weight,
        np.sin(backward) * weight,
    )
    return [jnp.asarray(table.astype(ml_dtypes.bfloat16)) for table in tables]


def smoothing_band(taps_ref, row_ref, width):
    row_ref[...] = jnp.zeros_like(row_ref)
    lead = width - (taps_ref.shape[1] - 1) // 2
    row_ref[:, lead : lead + taps_ref.shape[1]] = taps_ref[...]
    taps = row_ref[...].astype(BF16).astype(F32)
    band = pltpu.roll(
        jnp.broadcast_to(taps, (WIDE, row_ref.shape[1])), 0, 1, stride=1, stride_axis=0
    ).astype(BF16)
    return band, 1.0 / jnp.sum(taps)


def normalize(piece, pieces, rows, band, scale, unit_ref):
    width = unit_ref.shape[1] // pieces
    outside = jnp.zeros((rows, width), F32)
    for first in range(0, pieces, 2):
        parts = [piece(p) if 0 <= p < pieces else outside for p in range(first - 1, first + 3)]
        smoothed = lax.dot_general(
            jnp.abs(jnp.concatenate(parts, 1)).astype(BF16),
            band,
            (((1,), (1,)), ((), ())),
            preferred_element_type=F32,
        )
        values = jnp.concatenate(parts[1:3], 1)
        unit_ref[:, first * width : first * width + WIDE] = (
            values / (smoothed * scale + EPSILON)
        ).astype(BF16)


def fold(unit_ref, even_ref, odd_ref):
    mirror = (
        lax.broadcasted_iota(jnp.int32, (WIDE, WIDE), 0)
        + lax.broadcasted_iota(jnp.int32, (WIDE, WIDE), 1)
        == WIDE - 1
    ).astype(BF16)
    middle = even_ref.shape[1]
    for start in range(0, middle, WIDE):
        mirrored = jnp.dot(
            unit_ref[:, middle - start - WIDE : middle - start],
            mirror,
            preferred_element_type=F32,
        )
        later = unit_ref[:, middle + start : middle + start + WIDE].astype(F32)
        even_ref[:, start : start + WIDE] = (later + mirrored).astype(BF16)
        odd_ref[:, start : start + WIDE] = (later - mirrored).astype(BF16)


def own_kernel(
    raw_ref,
    taps_ref,
    cos_hbm,
    sin_hbm,
    own_cos_ref,
    own_sin_ref,
    cos_ref,
    sin_ref,
    band_ref,
    scale_ref,
    row_ref,
    unit_ref,
    even_ref,
    odd_ref,
    copied,
):
    pieces, rows, width = raw_ref.shape
    copies = [
        pltpu.make_async_copy(source, target, copied.at[place])
        for place, (source, target) in enumerate(((cos_hbm, cos_ref), (sin_hbm, sin_ref)))
    ]
    for copy in copies:
        copy.start()
    band, scale = smoothing_band(taps_ref, row_ref, width)
    band_ref[...] = band
    scale_ref[...] = jnp.broadcast_to(scale, scale_ref.shape)
    normalize(lambda p: raw_ref[p].astype(F32), pieces, rows, band, scale, unit_ref)
    fold(unit_ref, even_ref, odd_ref)
    spare = own_cos_ref.shape[1] - rows
    frequencies = cos_ref.shape[1]
    copies[0].wait()
    copies[1].wait()
    for part_ref, table_ref, spectrum_ref in (
        (even_ref, cos_ref, own_cos_ref),
        (odd_ref, sin_ref, own_sin_ref),
    ):
        for start in range(0, frequencies, WIDE):
            stop = min(start + WIDE, frequencies)
            spectrum = jnp.dot(
                part_ref[...], table_ref[:, start:stop], preferred_element_type=F32
            )
            for lane in range(start, stop, LANES):
                tile = spectrum[:, lane - start : lane - start + LANES]
                spectrum_ref[lane // LANES, :rows] = tile
                spectrum_ref[lane // LANES, rows:] = tile[:spare]


def own_spectra(records, smooth_taps, tables, spare):
    pieces, rows, width = records.shape
    samples = pieces * width
    frequencies = tables[0].shape[1]
    vmem = pl.BlockSpec(memory_space=pltpu.VMEM)
    hbm = pl.BlockSpec(memory_space=pltpu.HBM)
    spectrum = jax.ShapeDtypeStruct((frequencies // LANES, rows + spare, LANES), F32)
    return pl.pallas_call(
        own_kernel,
        out_shape=[spectrum, spectrum]
        + [jax.ShapeDtypeStruct(table.shape, BF16) for table in tables]
        + [
            jax.ShapeDtypeStruct((WIDE, 2 * WIDE), BF16),
            jax.ShapeDtypeStruct((1, WIDE), F32),
        ],
        in_specs=[vmem, vmem] + [hbm] * 2,
        out_specs=[vmem] * 6,
        scratch_shapes=[
            pltpu.VMEM((1, 2 * WIDE), F32),
            pltpu.VMEM((rows, samples), BF16),
            pltpu.VMEM((rows, samples // 2), BF16),
            pltpu.VMEM((rows, samples // 2), BF16),
            pltpu.SemaphoreType.DMA((2,)),
        ],
        compiler_params=pltpu.CompilerParams(vmem_limit_bytes=47 << 20),
    )(records, smooth_taps[None], *tables)


def far_kernel(
    start_ref,
    own_cos_ref,
    own_sin_ref,
    cos_ref,
    sin_ref,
    band_ref,
    scale_ref,
    *refs,
):
    run_refs = refs[:3]
    (
        back_cos_hbm,
        back_sin_hbm,
        out_ref,
        unit_ref,
        even_ref,
        odd_ref,
        far_cos_ref,
        far_sin_ref,
        real_ref,
        imag_ref,
        back_cos_ref,
        back_sin_ref,
        copied,
    ) = refs[3:]
    copies = [
        pltpu.make_async_copy(back_cos_hbm, back_cos_ref, copied.at[0]),
        pltpu.make_async_copy(back_sin_hbm, back_sin_ref, copied.at[1]),
    ]
    for copy in copies:
        copy.start()
    _, pieces, share, _ = run_refs[0].shape
    block_rows = share * pieces
    blocks = [(ref, place) for ref in run_refs for place in range(ref.shape[0])]
    rows = len(blocks) * share
    frequencies = cos_ref.shape[1]
    inside = (lax.axis_size("cable") + REACH - lax.axis_index("cable")) * share
    within = lax.broadcasted_iota(jnp.int32, (rows, run_refs[0].shape[3]), 0) < inside
    normalize(
        lambda p: jnp.where(
            within,
            jnp.concatenate([ref[place, p].astype(F32) for ref, place in blocks], 0),
            0.0,
        ),
        pieces,
        rows,
        band_ref[...],
        scale_ref[...],
        unit_ref,
    )
    fold(unit_ref, even_ref, odd_ref)
    for start in range(0, frequencies, WIDE):
        stop = min(start + WIDE, frequencies)
        far_cos_ref[:, start:stop] = jnp.dot(
            even_ref[...], cos_ref[:, start:stop], preferred_element_type=F32
        )
        far_sin_ref[:, start:stop] = jnp.dot(
            odd_ref[...], sin_ref[:, start:stop], preferred_element_type=F32
        )

    slots = start_ref.shape[0]
    first = lax.axis_index("pair") * share
    place = first + lax.broadcasted_iota(jnp.int32, (share, frequencies), 0)
    pair = []
    for slot in range(slots):
        start = start_ref[slot]
        live = (start >= 0).astype(F32)
        start = jnp.maximum(start, 0)
        block = lax.div(start, block_rows)
        offset = lax.rem(start, block_rows)
        lower = pl.ds(pl.multiple_of(block * share, share), share)
        upper = pl.ds(pl.multiple_of(block * share + share, share), share)
        own = pl.ds(lax.rem(first - offset + block_rows, block_rows), share)
        before = place >= offset
        far_cos = jnp.where(before, far_cos_ref[lower], far_cos_ref[upper]) * live
        far_sin = jnp.where(before, far_sin_ref[lower], far_sin_ref[upper]) * live
        tiles = range(frequencies // LANES)
        own_cos = jnp.concatenate([own_cos_ref[tile, own] for tile in tiles], 1)
        own_sin = jnp.concatenate([own_sin_ref[tile, own] for tile in tiles], 1)
        pair.append(
            (own_cos * far_cos + own_sin * far_sin, own_cos * far_sin - own_sin * far_cos)
        )
        if len(pair) * share == 16:
            begin = (slot + 1) * share - 16
            real_ref[begin : begin + 16] = jnp.concatenate([p[0] for p in pair], 0).astype(BF16)
            imag_ref[begin : begin + 16] = jnp.concatenate([p[1] for p in pair], 0).astype(BF16)
            pair = []
    for copy in copies:
        copy.wait()
    result = jnp.dot(real_ref[...], back_cos_ref[...], preferred_element_type=F32) + jnp.dot(
        imag_ref[...], back_sin_ref[...], preferred_element_type=F32
    )
    for slot in range(slots):
        out_ref[slot] = jnp.concatenate(
            [
                result[slot * share : (slot + 1) * share, lane : lane + LANES]
                for lane in range(0, LAG_PAD, LANES)
            ],
            0,
        ).astype(BF16)


def far_products(starts, own, runs, tables):
    _, pieces, share, width = runs[0].shape
    slots = starts.shape[0]
    samples = pieces * width
    rows = sum(run.shape[0] for run in runs) * share
    frequencies = own[2].shape[1]
    vmem = pl.BlockSpec(memory_space=pltpu.VMEM)
    smem = pl.BlockSpec(memory_space=pltpu.SMEM)
    hbm = pl.BlockSpec(memory_space=pltpu.HBM)
    return pl.pallas_call(
        far_kernel,
        out_shape=jax.ShapeDtypeStruct((slots, share * LAG_PAD // LANES, LANES), BF16),
        in_specs=[smem] + [vmem] * (len(own) + len(runs)) + [hbm] * 2,
        out_specs=vmem,
        scratch_shapes=[
            pltpu.VMEM((rows, samples), BF16),
            pltpu.VMEM((rows, samples // 2), BF16),
            pltpu.VMEM((rows, samples // 2), BF16),
            pltpu.VMEM((rows, frequencies), F32),
            pltpu.VMEM((rows, frequencies), F32),
            pltpu.VMEM((slots * share, frequencies), BF16),
            pltpu.VMEM((slots * share, frequencies), BF16),
            pltpu.VMEM(tables[0].shape, BF16),
            pltpu.VMEM(tables[1].shape, BF16),
            pltpu.SemaphoreType.DMA((2,)),
        ],
        compiler_params=pltpu.CompilerParams(vmem_limit_bytes=44 << 20),
    )(starts, *own, *runs, *tables)


def place_kernel(start_ref, sent_ref, out_hbm, out_ref, copied):
    senders, rows, lanes = sent_ref.shape
    share = rows * lanes // LAG_PAD
    block_rows = senders * share
    offset = lax.rem(jnp.maximum(start_ref[lax.axis_index("pair")], 0), block_rows)
    turn = lax.rem(block_rows - offset, block_rows)
    total = out_ref.shape[0]
    for step in range(LAG_PAD // lanes):
        values = jnp.concatenate(
            [
                sent_ref[sender].astype(F32)[step * share : (step + 1) * share]
                for sender in range(senders)
            ],
            0,
        ).T
        stop = min(total, (step + 1) * lanes)
        out_ref[step * lanes : stop] = pltpu.roll(values, turn, 1)[: stop - step * lanes]
    written = pltpu.make_async_copy(out_ref, out_hbm.at[:, 0], copied.at[0])
    written.start()
    written.wait()


def place_lags(starts, sent, rows):
    vmem = pl.BlockSpec(memory_space=pltpu.VMEM)
    smem = pl.BlockSpec(memory_space=pltpu.SMEM)
    hbm = pl.BlockSpec(memory_space=pltpu.HBM)
    return pl.pallas_call(
        place_kernel,
        out_shape=jax.ShapeDtypeStruct((2 * LAG + 1, 1, rows), F32),
        in_specs=[smem, vmem],
        out_specs=hbm,
        scratch_shapes=[
            pltpu.VMEM((2 * LAG + 1, rows), F32),
            pltpu.SemaphoreType.DMA((1,)),
        ],
        compiler_params=pltpu.CompilerParams(vmem_limit_bytes=8 << 20),
    )(starts, sent)


def from_behind(value, axis, steps, also=()):
    count = lax.axis_size(axis)
    first, last = (max(0, -steps), min(count, count - steps))
    pairs = [(source, source + steps) for source in range(first, last)]
    return lax.ppermute(value, axis, pairs + list(also))


def per_device(raw_strain, smooth_taps, partner_block, chan_offset, pair_count):
    rows = raw_strain.shape[0]
    share = rows // lax.axis_size("pair")
    first_block = lax.axis_index("cable") - REACH
    starts = (partner_block[0] - first_block) * rows + chan_offset[0]
    live = jnp.arange(starts.shape[0], dtype=jnp.int32) < pair_count
    starts = jnp.where(live, starts, -1)
    records = lax.all_gather(raw_strain, "pair", axis=0)
    records, starts = lax.optimization_barrier((records, starts))
    mine = lax.dynamic_slice_in_dim(records, lax.axis_index("pair") * share, share, 1)
    last = lax.axis_size("cable") - 1
    middle = jnp.stack([mine, from_behind(mine, "cable", -1, [(0, last)])], 0)
    lower = from_behind(middle, "cable", REACH, [(last, 1)])
    upper = from_behind(middle, "cable", -REACH)
    tables = transform_tables(records.shape[0] * records.shape[2])
    own = own_spectra(records, smooth_taps, tables[:2], share)
    products = far_products(starts, own, [lower, middle, upper], tables[2:])
    sent = lax.all_to_all(products, "pair", 0, 0)
    return place_lags(starts, sent, rows).reshape(1, 1, 2 * LAG + 1, rows)


def solution(mesh):
    in_specs = (P("cable", "pair"), P(), P("cable", None), P("cable", None), P("cable"))
    out_specs = P("cable", "pair", None, None)
    return jax.shard_map(
        per_device, mesh=mesh, in_specs=in_specs, out_specs=out_specs, check_vma=False
    )
```

time: 129 us -> 64.9 us (0.50)
  the two profiles are of different devices: /device:TPU:43 before, /device:TPU:31 now
where the time goes in v3:
time: 64.9 us; the launch traced here: 64.7 us
  blocking collectives  39.3 us (61%)
  starting transfers between devices  9.24 us (14%)
  Pallas kernels  8.51 us (13%)
  waiting for transfers between devices  5.49 us (8%)
  between operations  0.75 us (1%)
  other arithmetic  0.69 us (1%)
  local copies, waits for them, and re-layouts  0.69 us (1%)
    all_gather x1, blocking collectives, per_device(): records = lax.all_gather(raw_strain, 'pair', axis=0)  25.3 us
    all_to_all x1, blocking collectives, per_device(): sent = lax.all_to_all(products, 'pair', 0, 0)  14 us
    ppermute x3, starting transfers between devices, from_behind(): return lax.ppermute(value, axis, pairs + list(also))  9.24 us
    ppermute x3, waiting for transfers between devices, from_behind(): return lax.ppermute(value, axis, pairs + list(also))  5.49 us
    pallas_call x1, Pallas kernels, far_products(): pl.pallas_call(far_kernel, out_shape=jax.ShapeDtypeStruct((slots, share *...  3.57 us
    pallas_call x1, Pallas kernels, own_spectra(): pl.pallas_call(own_kernel, out_shape=[spectrum, spectrum] + [jax.ShapeDty...  3.51 us
    pallas_call x1, Pallas kernels, place_lags(): pl.pallas_call(place_kernel, out_shape=jax.ShapeDtypeStruct((2 * LAG + 1,...  1.43 us
  transfers between devices with their start and end apart: 3, of which 1 were waited for; matrix products, arithmetic and copies ran while one was open for 0% of the time, Pallas kernels for 5%

profile of v3, /device:TPU:31, one launch (start us, length us, event | category | flops | bytes accessed | tf_op | source)
XLA Modules:
  0.0 64.7 jit_solution(18280189915762023927)
XLA Ops:
  0.0 25.3 %all-gather = bf16[2048,128]{1,0:T(8,128)(2,1)S(1)} all-gather(bf16[128,128]{1,0:T(8,128)(2,1)} %param.9), channel_id=2, replica_groups=mesh['cable'=32,'pair'=16] {'pair'}, dimensions={0}, use_global_device_ids=true | all-gather | bytes 557056 | tf_op jit(solution)/shard_map/all_gather | solution.py:345
  26.0 0.7 %compare_select_fusion.start_ref = s32[16]{0:T(128)S(1)} fusion(s32[1,16]{1,0:T(1,128)} %param.12, s32[1,16]{1,0:T(1,128)} %param.11, s32[]{:T(128)S(6)} %sub.10, s32[]{:T(128)} %bitcast.11), kind=kLoop, calls=%fused_computation.1 | loop fusion | flops 80 | bytes 200 | tf_op jit(solution)/shard_map/jit(_where)/select_n | solution.py:344
  26.7 2.5 %collective-permute-start = (bf16[16,8,128]{2,1,0:T(8,128)(2,1)S(1)}, bf16[16,8,128]{2,1,0:T(8,128)(2,1)S(1)}, u32[]{:S(2)}, u32[]{:S(2)}) collective-permute-start(bf16[16,8,128]{2,1,0:T(8,128)(2,1)S(1)} %constant_dynamic-slice_fusion), channel_id=1, source_target_pairs={{16,0},{32,16},{48,32},{64,48},{80,64},{96,80},{112,96},{128,112},... | collective-permute-start | bytes 98312 | tf_op jit(solution)/shard_map/ppermute | solution.py:335
  29.2 5.5 %collective-permute-done = bf16[16,8,128]{2,1,0:T(8,128)(2,1)S(1)} collective-permute-done((bf16[16,8,128]{2,1,0:T(8,128)(2,1)S(1)}, bf16[16,8,128]{2,1,0:T(8,128)(2,1)S(1)}, u32[]{:S(2)}, u32[]{:S(2)}) %collective-permute-start) | collective-permute-done | bytes 32800 | tf_op jit(solution)/shard_map/ppermute | solution.py:335
  34.7 1.9 %collective-permute-start.1 = (bf16[2,16,8,128]{3,2,1,0:T(8,128)(2,1)S(1)}, bf16[2,16,8,128]{3,2,1,0:T(8,128)(2,1)S(1)}, u32[]{:S(2)}, u32[]{:S(2)}) collective-permute-start(bf16[2,16,8,128]{3,2,1,0:T(8,128)(2,1)S(1)} %pad_maximum_fusion.refs_1_), channel_id=1, source_target_pairs={{0,32},{16,48},{32,64},{48,80},{64,96},{80,112},{96,128},{112,144}... | collective-permute-start | bytes 196616 | tf_op jit(solution)/shard_map/ppermute | solution.py:335
  36.6 4.8 %collective-permute-start.2 = (bf16[2,16,8,128]{3,2,1,0:T(8,128)(2,1)S(1)}, bf16[2,16,8,128]{3,2,1,0:T(8,128)(2,1)S(1)}, u32[]{:S(2)}, u32[]{:S(2)}) collective-permute-start(bf16[2,16,8,128]{3,2,1,0:T(8,128)(2,1)S(1)} %pad_maximum_fusion.refs_1_), channel_id=1, source_target_pairs={{32,0},{48,16},{64,32},{80,48},{96,64},{112,80},{128,96},{144,112}... | collective-permute-start | bytes 196616 | tf_op jit(solution)/shard_map/ppermute | solution.py:335
  41.5 0.0 copy-start.2
  41.5 0.6 copy-done.2
  42.1 0.0 copy-start
  42.1 0.0 copy-start.1
  42.1 3.5 %shard_map.91 = (f32[9,136,128]{2,1,0:T(8,128)S(1)}, f32[9,136,128]{2,1,0:T(8,128)S(1)}, bf16[1024,1152]{1,0:T(8,128)(2,1)S(1)}, bf16[1024,1152]{1,0:T(8,128)(2,...) custom-call(bf16[16,128,128]{2,1,0:T(8,128)(2,1)S(1)} %bitcast.14, f32[1,101]{1,0:T(1,128)S(1)} %bitcast.15, ...), custom_call_target="tpu_custom_call" | custom-call | tf_op jit(solution)/shard_map/pallas_call | solution.py:138
  45.7 0.0 collective-permute-done.1.refs_0_
  45.7 0.0 collective-permute-done.2.refs_2_
  45.7 0.0 copy-done
  45.7 0.0 copy-done.1
  45.7 3.6 %shard_map.92 = bf16[16,32,128]{2,1,0:T(8,128)(2,1)S(1)} custom-call(s32[16]{0:T(128)S(1)} %compare_select_fusion.start_ref, f32[9,136,128]{2,1,0:T(8,128)S(1)} %get-tuple-element.15.own_cos_ref, f32[9,136,128]{2,1,0:T(8,128)S(1)} %get-tuple-element.16.own_sin_ref, bf16[1024,1152]{1,0:T(8,128)(2,1)S(1)} %get-tuple-element.17.cos_ref, ...), custom_call_target="tpu_custom_call" | custom-call | tf_op jit(solution)/shard_map/pallas_call | solution.py:271
  49.3 14.0 %all_to_all.5.sent_ref = bf16[16,32,128]{2,1,0:T(8,128)(2,1)S(1)} all-to-all(bf16[16,32,128]{2,1,0:T(8,128)(2,1)S(1)} %shard_map.92), channel_id=1, replica_groups=mesh['cable'=32,'pair'=16] {'pair'}, dimensions={0} | all-to-all | bytes 262144 | tf_op jit(solution)/shard_map/all_to_all | solution.py:355
  63.2 1.4 %shard_map.93 = f32[401,1,128]{2,1,0:T(1,128)} custom-call(s32[16]{0:T(128)S(1)} %compare_select_fusion.start_ref, bf16[16,32,128]{2,1,0:T(8,128)(2,1)S(1)} %all_to_all.5.sent_ref), custom_call_target="tpu_custom_call" | custom-call | tf_op jit(solution)/shard_map/pallas_call | solution.py:318
  (3 shorter events, 0.0 us)
Async XLA Ops:
  26.7 8.0 %collective-permute-start = (bf16[16,8,128]{2,1,0:T(8,128)(2,1)S(1)}, bf16[16,8,128]{2,1,0:T(8,128)(2,1)S(1)}, u32[]{:S(2)}, u32[]{:S(2)}) collective-permute-start(bf16[16,8,128]{2,1,0:T(8,128)(2,1)S(1)} %constant_dynamic-slice_fusion), channel_id=1, source_target_pairs={{16,0},{32,16},{48,32},{64,48},{80,64},{96,80},{112,96},{128,112},... | collective-permute-start | bytes 98312 | tf_op jit(solution)/shard_map/ppermute | solution.py:335
  34.7 11.0 %collective-permute-start.1 = (bf16[2,16,8,128]{3,2,1,0:T(8,128)(2,1)S(1)}, bf16[2,16,8,128]{3,2,1,0:T(8,128)(2,1)S(1)}, u32[]{:S(2)}, u32[]{:S(2)}) collective-permute-start(bf16[2,16,8,128]{3,2,1,0:T(8,128)(2,1)S(1)} %pad_maximum_fusion.refs_1_), channel_id=1, source_target_pairs={{0,32},{16,48},{32,64},{48,80},{64,96},{80,112},{96,128},{112,144}... | collective-permute-start | bytes 196616 | tf_op jit(solution)/shard_map/ppermute | solution.py:335
  36.6 9.1 %collective-permute-start.2 = (bf16[2,16,8,128]{3,2,1,0:T(8,128)(2,1)S(1)}, bf16[2,16,8,128]{3,2,1,0:T(8,128)(2,1)S(1)}, u32[]{:S(2)}, u32[]{:S(2)}) collective-permute-start(bf16[2,16,8,128]{3,2,1,0:T(8,128)(2,1)S(1)} %pad_maximum_fusion.refs_1_), channel_id=1, source_target_pairs={{32,0},{48,16},{64,32},{80,48},{96,64},{112,80},{128,96},{144,112}... | collective-permute-start | bytes 196616 | tf_op jit(solution)/shard_map/ppermute | solution.py:335
  41.5 0.7 %copy-start.2 = (f32[101]{0:T(128)S(1)}, f32[101]{0:T(128)}, u32[]{:S(2)}) copy-start(f32[101]{0:T(128)} %param.10) | copy-start | bytes 1216
  42.1 3.5 %copy-start = (bf16[1152,512]{1,0:T(8,128)(2,1)S(1)}, bf16[1152,512]{1,0:T(8,128)(2,1)}, u32[]{:S(2)}) copy-start(bf16[1152,512]{1,0:T(8,128)(2,1)} %constant.31.clone.refs_3_) | copy-start | bytes 3538948
  42.1 3.6 %copy-start.1 = (bf16[1152,512]{1,0:T(8,128)(2,1)S(1)}, bf16[1152,512]{1,0:T(8,128)(2,1)}, u32[]{:S(2)}) copy-start(bf16[1152,512]{1,0:T(8,128)(2,1)} %constant.32.clone.refs_4_) | copy-start | bytes 3538948

commit v4 on v3

v4 whole, which is shorter than its diff:
```python
import math

import jax
import jax.numpy as jnp
import ml_dtypes
import numpy as np
from jax import lax
from jax.experimental import pallas as pl
from jax.experimental.pallas import tpu as pltpu
from jax.sharding import PartitionSpec as P

LAG = 200
REACH = 2
EPSILON = 1e-05
WIDE = 256
LAG_PAD = 512
LANES = 128
TABLE_LIMIT = 47
OWN_LIMIT = 44
FAR_LIMIT = 44
F32 = jnp.float32
BF16 = jnp.bfloat16


def transform_tables(samples):
    length = -(-(samples + LAG) // WIDE) * WIDE
    theta = 2 * np.pi * (np.arange(length // 2) + 0.5) / length
    forward = np.outer(np.arange(samples // 2) + 0.5, theta)
    backward = np.outer(theta, np.arange(LAG_PAD) - LAG)
    weight = 2.0 / length / math.sqrt(samples)
    tables = (
        np.cos(forward),
        np.sin(forward),
        np.cos(backward) * weight,
        np.sin(backward) * weight,
    )
    return [jnp.asarray(table.astype(ml_dtypes.bfloat16)) for table in tables]


def smoothing_band(row):
    taps = row.astype(BF16).astype(F32)
    band = pltpu.roll(
        jnp.broadcast_to(taps, (WIDE, row.shape[1])), 0, 1, stride=1, stride_axis=0
    ).astype(BF16)
    return band, 1.0 / jnp.sum(taps)


def normalize(parts, band, scale):
    rows, width = parts[0].shape
    outside = jnp.zeros((rows, width), F32)
    padded = [outside] + parts + [outside]
    firsts = range(0, len(parts), 2)
    smoothed = lax.dot_general(
        jnp.concatenate(
            [jnp.abs(jnp.concatenate(padded[p : p + 4], 1)).astype(BF16) for p in firsts], 0
        ),
        band,
        (((1,), (1,)), ((), ())),
        preferred_element_type=F32,
    )
    values = jnp.concatenate([jnp.concatenate(parts[p : p + 2], 1) for p in firsts], 0)
    return (values / (smoothed * scale + EPSILON)).astype(BF16)


def fold(unit, rows):
    mirror = (
        lax.broadcasted_iota(jnp.int32, (WIDE, WIDE), 0)
        + lax.broadcasted_iota(jnp.int32, (WIDE, WIDE), 1)
        == WIDE - 1
    ).astype(BF16)
    half = unit.shape[0] // 2
    mirrored = jnp.dot(unit[:half], mirror, preferred_element_type=F32)
    later = unit[half:].astype(F32)
    even, odd = [], []
    for start in range(0, half, rows):
        ahead = later[start : start + rows]
        behind = mirrored[half - start - rows : half - start]
        even.append((ahead + behind).astype(BF16))
        odd.append((ahead - behind).astype(BF16))
    return jnp.concatenate(even, 1), jnp.concatenate(odd, 1)


def table_kernel(
    row_ref, cos_hbm, sin_hbm, cos_ref, sin_ref, band_ref, scale_ref, copied
):
    copies = [
        pltpu.make_async_copy(cos_hbm, cos_ref, copied.at[0]),
        pltpu.make_async_copy(sin_hbm, sin_ref, copied.at[1]),
    ]
    for copy in copies:
        copy.start()
    band, scale = smoothing_band(row_ref[...])
    band_ref[...] = band
    scale_ref[...] = jnp.broadcast_to(scale, scale_ref.shape)
    for copy in copies:
        copy.wait()


def forward_tables(taps_row, tables):
    vmem = pl.BlockSpec(memory_space=pltpu.VMEM)
    hbm = pl.BlockSpec(memory_space=pltpu.HBM)
    return pl.pallas_call(
        table_kernel,
        out_shape=[jax.ShapeDtypeStruct(table.shape, BF16) for table in tables]
        + [
            jax.ShapeDtypeStruct((WIDE, 2 * WIDE), BF16),
            jax.ShapeDtypeStruct((1, WIDE), F32),
        ],
        in_specs=[vmem, hbm, hbm],
        out_specs=[vmem] * 4,
        scratch_shapes=[pltpu.SemaphoreType.DMA((2,))],
        compiler_params=pltpu.CompilerParams(vmem_limit_bytes=TABLE_LIMIT << 20),
    )(taps_row, *tables)


def own_kernel(
    raw_ref, cos_ref, sin_ref, band_ref, scale_ref, own_cos_ref, own_sin_ref
):
    pieces, rows, _ = raw_ref.shape
    even, odd = fold(
        normalize(
            [raw_ref[p].astype(F32) for p in range(pieces)], band_ref[...], scale_ref[...]
        ),
        rows,
    )
    spare = own_cos_ref.shape[1] - rows
    frequencies = cos_ref.shape[1]
    for part, table_ref, spectrum_ref in (
        (even, cos_ref, own_cos_ref),
        (odd, sin_ref, own_sin_ref),
    ):
        for start in range(0, frequencies, WIDE):
            stop = min(start + WIDE, frequencies)
            spectrum = jnp.dot(part, table_ref[:, start:stop], preferred_element_type=F32)
            for lane in range(start, stop, LANES):
                tile = spectrum[:, lane - start : lane - start + LANES]
                spectrum_ref[lane // LANES, :rows] = tile
                spectrum_ref[lane // LANES, rows:] = tile[:spare]


def own_spectra(records, shared, spare):
    rows = records.shape[1]
    frequencies = shared[0].shape[1]
    vmem = pl.BlockSpec(memory_space=pltpu.VMEM)
    spectrum = jax.ShapeDtypeStruct((frequencies // LANES, rows + spare, LANES), F32)
    return pl.pallas_call(
        own_kernel,
        out_shape=[spectrum, spectrum],
        in_specs=[vmem] * (1 + len(shared)),
        out_specs=[vmem] * 2,
        compiler_params=pltpu.CompilerParams(vmem_limit_bytes=OWN_LIMIT << 20),
    )(records, *shared)


def far_kernel(
    start_any,
    own_cos_ref,
    own_sin_ref,
    cos_ref,
    sin_ref,
    band_ref,
    scale_ref,
    *refs,
):
    run_refs = refs[:3]
    (
        back_cos_hbm,
        back_sin_hbm,
        out_ref,
        far_cos_ref,
        far_sin_ref,
        real_ref,
        imag_ref,
        back_cos_ref,
        back_sin_ref,
        start_ref,
        copied,
    ) = refs[3:]
    start_copy = pltpu.make_async_copy(start_any, start_ref, copied.at[2])
    start_copy.start()
    copies = [
        pltpu.make_async_copy(back_cos_hbm, back_cos_ref, copied.at[0]),
        pltpu.make_async_copy(back_sin_hbm, back_sin_ref, copied.at[1]),
    ]
    for copy in copies:
        copy.start()
    _, pieces, share, _ = run_refs[0].shape
    block_rows = share * pieces
    blocks = [(ref, place) for ref in run_refs for place in range(ref.shape[0])]
    rows = len(blocks) * share
    frequencies = cos_ref.shape[1]
    inside = (lax.axis_size("cable") + REACH - lax.axis_index("cable")) * share
    within = lax.broadcasted_iota(jnp.int32, (rows, run_refs[0].shape[3]), 0) < inside
    parts = [
        jnp.where(
            within,
            jnp.concatenate([ref[place, p].astype(F32) for ref, place in blocks], 0),
            0.0,
        )
        for p in range(pieces)
    ]
    even, odd = fold(normalize(parts, band_ref[...], scale_ref[...]), rows)
    for start in range(0, frequencies, WIDE):
        stop = min(start + WIDE, frequencies)
        far_cos_ref[:, start:stop] = jnp.dot(
            even, cos_ref[:, start:stop], preferred_element_type=F32
        )
        far_sin_ref[:, start:stop] = jnp.dot(
            odd, sin_ref[:, start:stop], preferred_element_type=F32
        )

    slots = start_ref.shape[0]
    first = lax.axis_index("pair") * share
    place = first + lax.broadcasted_iota(jnp.int32, (share, frequencies), 0)
    pair = []
    start_copy.wait()
    for slot in range(slots):
        start = jnp.maximum(start_ref[slot], 0)
        block = lax.div(start, block_rows)
        offset = lax.rem(start, block_rows)
        lower = pl.ds(pl.multiple_of(block * share, share), share)
        upper = pl.ds(pl.multiple_of(block * share + share, share), share)
        own = pl.ds(lax.rem(first - offset + block_rows, block_rows), share)
        before = place >= offset
        far_cos = jnp.where(before, far_cos_ref[lower], far_cos_ref[upper])
        far_sin = jnp.where(before, far_sin_ref[lower], far_sin_ref[upper])
        tiles = range(frequencies // LANES)
        own_cos = jnp.concatenate([own_cos_ref[tile, own] for tile in tiles], 1)
        own_sin = jnp.concatenate([own_sin_ref[tile, own] for tile in tiles], 1)
        pair.append(
            (own_cos * far_cos + own_sin * far_sin, own_cos * far_sin - own_sin * far_cos)
        )
        if len(pair) * share == 16:
            begin = (slot + 1) * share - 16
            real_ref[begin : begin + 16] = jnp.concatenate([p[0] for p in pair], 0).astype(BF16)
            imag_ref[begin : begin + 16] = jnp.concatenate([p[1] for p in pair], 0).astype(BF16)
            pair = []
    for copy in copies:
        copy.wait()
    result = jnp.dot(real_ref[...], back_cos_ref[...], preferred_element_type=F32) + jnp.dot(
        imag_ref[...], back_sin_ref[...], preferred_element_type=F32
    )
    tile = (share * LAG_PAD // LANES, LANES)
    last_lane = (lax.broadcasted_iota(jnp.int32, tile, 0) >= tile[0] - share) & (
        lax.broadcasted_iota(jnp.int32, tile, 1) == LANES - 1
    )
    for slot in range(slots):
        lags = jnp.concatenate(
            [
                result[slot * share : (slot + 1) * share, lane : lane + LANES]
                for lane in range(0, LAG_PAD, LANES)
            ],
            0,
        )
        start = start_ref[slot]
        offset = lax.rem(jnp.maximum(start, 0), block_rows).astype(F32)
        lags = jnp.where(start >= 0, lags, 0.0)
        out_ref[slot] = jnp.where(last_lane, offset, lags).astype(BF16)


def far_products(starts, own, runs, tables):
    share = runs[0].shape[2]
    slots = starts.shape[0]
    rows = sum(run.shape[0] for run in runs) * share
    frequencies = own[2].shape[1]
    vmem = pl.BlockSpec(memory_space=pltpu.VMEM)
    hbm = pl.BlockSpec(memory_space=pltpu.HBM)
    anywhere = pl.BlockSpec(memory_space=pl.ANY)
    return pl.pallas_call(
        far_kernel,
        out_shape=jax.ShapeDtypeStruct((slots, share * LAG_PAD // LANES, LANES), BF16),
        in_specs=[anywhere] + [vmem] * (len(own) + len(runs)) + [hbm] * 2,
        out_specs=vmem,
        scratch_shapes=[
            pltpu.VMEM((rows, frequencies), F32),
            pltpu.VMEM((rows, frequencies), F32),
            pltpu.VMEM((slots * share, frequencies), BF16),
            pltpu.VMEM((slots * share, frequencies), BF16),
            pltpu.VMEM(tables[0].shape, BF16),
            pltpu.VMEM(tables[1].shape, BF16),
            pltpu.SMEM((slots,), jnp.int32),
            pltpu.SemaphoreType.DMA((3,)),
        ],
        compiler_params=pltpu.CompilerParams(vmem_limit_bytes=FAR_LIMIT << 20),
    )(starts, *own, *runs, *tables)


def place_kernel(sent_ref, out_hbm, out_ref, copied):
    senders, rows, lanes = sent_ref.shape
    tiles = LAG_PAD // lanes
    share = rows // tiles
    values = [sent_ref[sender].astype(F32) for sender in range(senders)]
    lags = [
        jnp.concatenate([value[step * share : (step + 1) * share] for value in values], 0)
        for step in range(tiles)
    ]
    block_rows = senders * share
    row = lax.broadcasted_iota(jnp.int32, (block_rows, block_rows), 0)
    channel = lax.broadcasted_iota(jnp.int32, (block_rows, block_rows), 1)
    offset = lags[-1][:, lanes - 1 :].astype(jnp.int32)
    ahead = row - offset - channel
    turn = ((ahead == 0) | (ahead == -block_rows)).astype(BF16)
    total = out_ref.shape[0]
    written = []
    for step in range(tiles):
        span = pl.ds(step * lanes, min(total, (step + 1) * lanes) - step * lanes)
        out_ref[span] = lax.dot_general(
            lags[step].astype(BF16),
            turn,
            (((0,), (0,)), ((), ())),
            preferred_element_type=F32,
        )[: span.size]
        written.append(
            pltpu.make_async_copy(out_ref.at[span], out_hbm.at[span, 0], copied.at[step])
        )
        written[-1].start()
    for copy in written:
        copy.wait()


def place_lags(sent, rows):
    vmem = pl.BlockSpec(memory_space=pltpu.VMEM)
    hbm = pl.BlockSpec(memory_space=pltpu.HBM)
    return pl.pallas_call(
        place_kernel,
        out_shape=jax.ShapeDtypeStruct((2 * LAG + 1, 1, rows), F32),
        in_specs=[vmem],
        out_specs=hbm,
        scratch_shapes=[
            pltpu.VMEM((2 * LAG + 1, rows), F32),
            pltpu.SemaphoreType.DMA((LAG_PAD // LANES,)),
        ],
        compiler_params=pltpu.CompilerParams(vmem_limit_bytes=8 << 20),
    )(sent)


def from_behind(value, axis, steps, also=()):
    count = lax.axis_size(axis)
    first, last = (max(0, -steps), min(count, count - steps))
    pairs = [(source, source + steps) for source in range(first, last)]
    return lax.ppermute(value, axis, pairs + list(also))


def per_device(raw_strain, smooth_taps, partner_block, chan_offset, pair_count):
    rows = raw_strain.shape[0]
    share = rows // lax.axis_size("pair")
    first_block = lax.axis_index("cable") - REACH
    records = lax.all_gather(raw_strain, "pair", axis=0)
    mine = lax.dynamic_slice_in_dim(records, lax.axis_index("pair") * share, share, 1)
    tables = transform_tables(records.shape[0] * records.shape[2])
    mine, smooth_taps, partner_block, chan_offset, pair_count = lax.optimization_barrier(
        (mine, smooth_taps, partner_block, chan_offset, pair_count)
    )
    last = lax.axis_size("cable") - 1
    middle = jnp.stack([mine, from_behind(mine, "cable", -1, [(0, last)])], 0)
    starts = (partner_block[0] - first_block) * rows + chan_offset[0]
    live = jnp.arange(starts.shape[0], dtype=jnp.int32) < pair_count
    starts = jnp.where(live, starts, -1)
    lead = records.shape[2] - (smooth_taps.shape[0] - 1) // 2
    taps_row = jnp.pad(smooth_taps, (lead, 2 * WIDE - lead - smooth_taps.shape[0]))[None]
    middle, starts, taps_row = lax.optimization_barrier((middle, starts, taps_row))
    shared = forward_tables(taps_row, tables[:2])
    lower = from_behind(middle, "cable", REACH, [(last, 1)])
    upper = from_behind(middle, "cable", -REACH)
    own = own_spectra(records, shared, share)
    products = far_products(starts, [*own, *shared], [lower, middle, upper], tables[2:])
    sent = lax.all_to_all(products, "pair", 0, 0)
    return place_lags(sent, rows).reshape(1, 1, 2 * LAG + 1, rows)


def solution(mesh):
    in_specs = (P("cable", "pair"), P(), P("cable", None), P("cable", None), P("cable"))
    out_specs = P("cable", "pair", None, None)
    return jax.shard_map(
        per_device, mesh=mesh, in_specs=in_specs, out_specs=out_specs, check_vma=False
    )
```

time: 64.9 us -> 62.3 us (0.960)
  waiting for transfers between devices: 5.49 us -> 3.46 us
    ppermute x3, waiting for transfers between devices: 5.49 us -> 3.46 us  [from_behind(): return lax.ppermute(value, axis, pairs + list(also))]
    pallas_call x1, Pallas kernels: 3.57 us -> 2.78 us  [far_products(): pl.pallas_call(far_kernel, out_shape=jax.ShapeDtypeStruct((slots, share *...]
    pad x0 -> x1, local copies, waits for them, and re-layouts: none -> 0.73 us  [per_device(): jnp.pad(smooth_taps, (lead, 2 * WIDE - lead - smooth_taps.shape[0]))[None]]
    pallas_call x1 -> x2, Pallas kernels: 3.51 us -> 4.17 us  [the longest x1 2.4 us: forward_tables(): pl.pallas_call(table_kernel, out_shape=[jax.ShapeDtypeStruct(table.shape,...]
  transfers between devices with their start and end apart: 3 -> 3, of which waited for: 1 -> 1; matrix products, arithmetic and copies ran while one was open for 0% -> 2% of each run, Pallas kernels for 5% -> 7%
where the time goes in v4:
time: 62.3 us; the launch traced here: 62.1 us
  blocking collectives  39.3 us (63%)
  starting transfers between devices  9.24 us (15%)
  Pallas kernels  7.88 us (13%)
  waiting for transfers between devices  3.46 us (6%)
  local copies, waits for them, and re-layouts  0.75 us (1%)
  between operations  0.75 us (1%)
  other arithmetic  0.69 us (1%)
    all_gather x1, blocking collectives, per_device(): records = lax.all_gather(raw_strain, 'pair', axis=0)  25.3 us
    all_to_all x1, blocking collectives, per_device(): sent = lax.all_to_all(products, 'pair', 0, 0)  13.9 us
    ppermute x3, starting transfers between devices, from_behind(): return lax.ppermute(value, axis, pairs + list(also))  9.24 us
    ppermute x3, waiting for transfers between devices, from_behind(): return lax.ppermute(value, axis, pairs + list(also))  3.46 us
    pallas_call x1, Pallas kernels, far_products(): pl.pallas_call(far_kernel, out_shape=jax.ShapeDtypeStruct((slots, share *...  2.78 us
    pallas_call x1, Pallas kernels, forward_tables(): pl.pallas_call(table_kernel, out_shape=[jax.ShapeDtypeStruct(table.shape,...  2.4 us
    pallas_call x1, Pallas kernels, own_spectra(): pl.pallas_call(own_kernel, out_shape=[spectrum, spectrum], in_specs=[vmem...  1.76 us
  transfers between devices with their start and end apart: 3, of which 1 were waited for; matrix products, arithmetic and copies ran while one was open for 2% of the time, Pallas kernels for 7%

profile of v4, /device:TPU:31, one launch (start us, length us, event | category | flops | bytes accessed | tf_op | source)
XLA Modules:
  0.0 62.1 jit_solution(8825878422103559815)
XLA Ops:
  0.0 25.3 %all-gather = bf16[2048,128]{1,0:T(8,128)(2,1)S(1)} all-gather(bf16[128,128]{1,0:T(8,128)(2,1)} %param.9), channel_id=2, replica_groups=mesh['cable'=32,'pair'=16] {'pair'}, dimensions={0}, use_global_device_ids=true | all-gather | bytes 557056 | tf_op jit(solution)/shard_map/all_gather | solution.py:348
  25.3 2.5 %collective-permute-start = (bf16[16,8,128]{2,1,0:T(8,128)(2,1)S(1)}, bf16[16,8,128]{2,1,0:T(8,128)(2,1)S(1)}, u32[]{:S(2)}, u32[]{:S(2)}) collective-permute-start(bf16[16,8,128]{2,1,0:T(8,128)(2,1)S(1)} %constant_dynamic-slice_fusion), channel_id=1, source_target_pairs={{16,0},{32,16},{48,32},{64,48},{80,64},{96,80},{112,96},{128,112},... | collective-permute-start | bytes 98312 | tf_op jit(solution)/shard_map/ppermute | solution.py:341
  28.5 0.7 %compare_select_fusion.start_any = s32[16]{0:T(128)S(1)} fusion(s32[1,16]{1,0:T(1,128)} %param.12, s32[1,16]{1,0:T(1,128)} %param.11, s32[]{:T(128)S(6)} %sub.10, s32[]{:T(128)} %bitcast.10), kind=kLoop, calls=%fused_computation.1 | loop fusion | flops 80 | bytes 200 | tf_op jit(solution)/shard_map/jit(_where)/select_n | solution.py:358
  29.1 0.7 %pad.4 = f32[512]{0:T(512)S(1)} pad(f32[101]{0:T(128)} %param.10, f32[]{:T(128)} %constant.30.clone.1), padding=78_333 | pad | bytes 2456 | tf_op jit(solution)/shard_map/jit(_pad)/pad | solution.py:360
  29.9 3.5 %collective-permute-done = bf16[16,8,128]{2,1,0:T(8,128)(2,1)S(1)} collective-permute-done((bf16[16,8,128]{2,1,0:T(8,128)(2,1)S(1)}, bf16[16,8,128]{2,1,0:T(8,128)(2,1)S(1)}, u32[]{:S(2)}, u32[]{:S(2)}) %collective-permute-start) | collective-permute-done | bytes 32800 | tf_op jit(solution)/shard_map/ppermute | solution.py:341
  33.3 1.9 %collective-permute-start.1 = (bf16[2,16,8,128]{3,2,1,0:T(8,128)(2,1)S(1)}, bf16[2,16,8,128]{3,2,1,0:T(8,128)(2,1)S(1)}, u32[]{:S(2)}, u32[]{:S(2)}) collective-permute-start(bf16[2,16,8,128]{3,2,1,0:T(8,128)(2,1)S(1)} %pad_maximum_fusion.refs_1_), channel_id=1, source_target_pairs={{0,32},{16,48},{32,64},{48,80},{64,96},{80,112},{96,128},{112,144}... | collective-permute-start | bytes 196616 | tf_op jit(solution)/shard_map/ppermute | solution.py:341
  35.3 4.8 %collective-permute-start.2 = (bf16[2,16,8,128]{3,2,1,0:T(8,128)(2,1)S(1)}, bf16[2,16,8,128]{3,2,1,0:T(8,128)(2,1)S(1)}, u32[]{:S(2)}, u32[]{:S(2)}) collective-permute-start(bf16[2,16,8,128]{3,2,1,0:T(8,128)(2,1)S(1)} %pad_maximum_fusion.refs_1_), channel_id=1, source_target_pairs={{32,0},{48,16},{64,32},{80,48},{96,64},{112,80},{128,96},{144,112}... | collective-permute-start | bytes 196616 | tf_op jit(solution)/shard_map/ppermute | solution.py:341
  40.1 2.4 %shard_map.91 = (bf16[1024,1152]{1,0:T(8,128)(2,1)S(1)}, bf16[1024,1152]{1,0:T(8,128)(2,1)S(1)}, bf16[256,512]{1,0:T(8,128)(2,1)S(1)}, f32[1,256]{1,0:T(1,128)S(1)}) custom-call(f32[1,512]{1,0:T(1,128)S(1)} %bitcast.13, bf16[1024,1152]{1,0:T(8,128)(2,1)} %constant.31.clone.cos_hbm, bf16[1024,1152]{1,0:T(8,128)(2,1)} %constant.32.clone.sin_hbm), custom_call_target="tpu_custom_call" | custom-call | tf_op jit(solution)/shard_map/pallas_call | solution.py:102
  42.5 0.0 copy-start
  42.6 0.0 copy-start.1
  42.6 1.8 %shard_map.92 = (f32[9,136,128]{2,1,0:T(8,128)S(1)}, f32[9,136,128]{2,1,0:T(8,128)S(1)}) custom-call(bf16[16,128,128]{2,1,0:T(8,128)(2,1)S(1)} %bitcast.12, bf16[1024,1152]{1,0:T(8,128)(2,1)S(1)} %get-tuple-element.26.cos_ref, bf16[1024,1152]{1,0:T(8,128)(2,1)S(1)} %get-tuple-element.27.sin_ref, bf16[256,512]{1,0:T(8,128)(2,1)S(1)} %get-tuple-element.28.band_ref, ...), custom_call_target="tpu_custom_call" | custom-call | tf_op jit(solution)/shard_map/pallas_call | solution.py:146
  44.3 0.0 collective-permute-done.1.refs_0_
  44.4 0.0 collective-permute-done.2.refs_2_
  44.4 0.0 copy-done
  44.4 0.0 copy-done.1
  44.4 2.8 %shard_map.93 = bf16[16,32,128]{2,1,0:T(8,128)(2,1)S(1)} custom-call(s32[16]{0:T(128)S(1)} %compare_select_fusion.start_any, f32[9,136,128]{2,1,0:T(8,128)S(1)} %get-tuple-element.30.own_cos_ref, f32[9,136,128]{2,1,0:T(8,128)S(1)} %get-tuple-element.31.own_sin_ref, bf16[1024,1152]{1,0:T(8,128)(2,1)S(1)} %get-tuple-element.26.cos_ref, ...), custom_call_target="tpu_custom_call" | custom-call | tf_op jit(solution)/shard_map/pallas_call | solution.py:269
  47.2 13.9 %all_to_all.5.sent_ref = bf16[16,32,128]{2,1,0:T(8,128)(2,1)S(1)} all-to-all(bf16[16,32,128]{2,1,0:T(8,128)(2,1)S(1)} %shard_map.93), channel_id=1, replica_groups=mesh['cable'=32,'pair'=16] {'pair'}, dimensions={0} | all-to-all | bytes 262144 | tf_op jit(solution)/shard_map/all_to_all | solution.py:367
  61.1 0.9 %shard_map.94 = f32[401,1,128]{2,1,0:T(1,128)} custom-call(bf16[16,32,128]{2,1,0:T(8,128)(2,1)S(1)} %all_to_all.5.sent_ref), custom_call_target="tpu_custom_call" | custom-call | tf_op jit(solution)/shard_map/pallas_call | solution.py:324
  (2 shorter events, 0.0 us)
Async XLA Ops:
  25.3 8.0 %collective-permute-start = (bf16[16,8,128]{2,1,0:T(8,128)(2,1)S(1)}, bf16[16,8,128]{2,1,0:T(8,128)(2,1)S(1)}, u32[]{:S(2)}, u32[]{:S(2)}) collective-permute-start(bf16[16,8,128]{2,1,0:T(8,128)(2,1)S(1)} %constant_dynamic-slice_fusion), channel_id=1, source_target_pairs={{16,0},{32,16},{48,32},{64,48},{80,64},{96,80},{112,96},{128,112},... | collective-permute-start | bytes 98312 | tf_op jit(solution)/shard_map/ppermute | solution.py:341
  33.3 11.0 %collective-permute-start.1 = (bf16[2,16,8,128]{3,2,1,0:T(8,128)(2,1)S(1)}, bf16[2,16,8,128]{3,2,1,0:T(8,128)(2,1)S(1)}, u32[]{:S(2)}, u32[]{:S(2)}) collective-permute-start(bf16[2,16,8,128]{3,2,1,0:T(8,128)(2,1)S(1)} %pad_maximum_fusion.refs_1_), channel_id=1, source_target_pairs={{0,32},{16,48},{32,64},{48,80},{64,96},{80,112},{96,128},{112,144}... | collective-permute-start | bytes 196616 | tf_op jit(solution)/shard_map/ppermute | solution.py:341
  35.3 9.1 %collective-permute-start.2 = (bf16[2,16,8,128]{3,2,1,0:T(8,128)(2,1)S(1)}, bf16[2,16,8,128]{3,2,1,0:T(8,128)(2,1)S(1)}, u32[]{:S(2)}, u32[]{:S(2)}) collective-permute-start(bf16[2,16,8,128]{3,2,1,0:T(8,128)(2,1)S(1)} %pad_maximum_fusion.refs_1_), channel_id=1, source_target_pairs={{32,0},{48,16},{64,32},{80,48},{96,64},{112,80},{128,96},{144,112}... | collective-permute-start | bytes 196616 | tf_op jit(solution)/shard_map/ppermute | solution.py:341
  42.5 1.8 %copy-start = (bf16[1152,512]{1,0:T(8,128)(2,1)S(1)}, bf16[1152,512]{1,0:T(8,128)(2,1)}, u32[]{:S(2)}) copy-start(bf16[1152,512]{1,0:T(8,128)(2,1)} %constant.33.clone.refs_3_) | copy-start | bytes 3538948
  42.6 1.8 %copy-start.1 = (bf16[1152,512]{1,0:T(8,128)(2,1)S(1)}, bf16[1152,512]{1,0:T(8,128)(2,1)}, u32[]{:S(2)}) copy-start(bf16[1152,512]{1,0:T(8,128)(2,1)} %constant.34.clone.refs_4_) | copy-start | bytes 3538948

commit v5 on v4

--- a/solution.py
+++ b/solution.py
@@ -15,25 +15,21 @@
 WIDE = 256
 LAG_PAD = 512
 LANES = 128
-TABLE_LIMIT = 47
-OWN_LIMIT = 44
+OWN_LIMIT = 49
 FAR_LIMIT = 44
 F32 = jnp.float32
 BF16 = jnp.bfloat16
 
 
 def transform_tables(samples):
-    length = -(-(samples + LAG) // WIDE) * WIDE
-    theta = 2 * np.pi * (np.arange(length // 2) + 0.5) / length
+    length = -(-(samples + LAG) // (4 * LANES)) * 4 * LANES
+    theta = 2 * np.pi * (np.arange(length // 4) + 0.5) / length
     forward = np.outer(np.arange(samples // 2) + 0.5, theta)
-    backward = np.outer(theta, np.arange(LAG_PAD) - LAG)
     weight = 2.0 / length / math.sqrt(samples)
-    tables = (
-        np.cos(forward),
-        np.sin(forward),
-        np.cos(backward) * weight,
-        np.sin(backward) * weight,
-    )
+    tables = [np.cos(forward), np.sin(forward)]
+    for first in (0, 1):
+        backward = np.outer(theta, np.arange(LAG_PAD // 2) * 2 + first - LAG)
+        tables += [np.cos(backward) * weight, np.sin(backward) * weight]
     return [jnp.asarray(table.astype(ml_dtypes.bfloat16)) for table in tables]
 
 
@@ -77,12 +73,26 @@
         behind = mirrored[half - start - rows : half - start]
         even.append((ahead + behind).astype(BF16))
         odd.append((ahead - behind).astype(BF16))
-    return jnp.concatenate(even, 1), jnp.concatenate(odd, 1)
-
-
-def table_kernel(
-    row_ref, cos_hbm, sin_hbm, cos_ref, sin_ref, band_ref, scale_ref, copied
+    even, odd = jnp.concatenate(even, 1), jnp.concatenate(odd, 1)
+    sign = 1 - 2 * lax.rem(lax.broadcasted_iota(jnp.int32, even.shape, 1), 2)
+    sign = sign.astype(F32).astype(BF16)
+    return jnp.concatenate([even, odd * sign], 0), jnp.concatenate([odd, even * sign], 0)
+
+
+def own_kernel(
+    raw_ref,
+    row_ref,
+    cos_hbm,
+    sin_hbm,
+    own_cos_ref,
+    own_sin_ref,
+    cos_ref,
+    sin_ref,
+    band_ref,
+    scale_ref,
+    copied,
 ):
+    pieces, rows, _ = raw_ref.shape
     copies = [
         pltpu.make_async_copy(cos_hbm, cos_ref, copied.at[0]),
         pltpu.make_async_copy(sin_hbm, sin_ref, copied.at[1]),
@@ -92,64 +102,44 @@
     band, scale = smoothing_band(row_ref[...])
     band_ref[...] = band
     scale_ref[...] = jnp.broadcast_to(scale, scale_ref.shape)
-    for copy in copies:
+    for_cos, for_sin = fold(
+        normalize([raw_ref[p].astype(F32) for p in range(pieces)], band, scale), rows
+    )
+    spare = own_cos_ref.shape[1] - rows
+    tiles = cos_ref.shape[1] // LANES
+    for copy, part, table_ref, lower_ref, upper_ref in (
+        (copies[0], for_cos, cos_ref, own_cos_ref, own_sin_ref),
+        (copies[1], for_sin, sin_ref, own_sin_ref, own_cos_ref),
+    ):
         copy.wait()
-
-
-def forward_tables(taps_row, tables):
+        spectrum = jnp.dot(part, table_ref[...], preferred_element_type=F32)
+        for tile in range(tiles):
+            lanes = spectrum[:, tile * LANES : (tile + 1) * LANES]
+            lower_ref[tile, :rows] = lanes[:rows]
+            lower_ref[tile, rows:] = lanes[:spare]
+            upper_ref[tiles + tile, :rows] = lanes[rows:]
+            upper_ref[tiles + tile, rows:] = lanes[rows : rows + spare]
+
+
+def own_spectra(records, taps_row, tables, spare):
+    rows = records.shape[1]
+    frequencies = 2 * tables[0].shape[1]
     vmem = pl.BlockSpec(memory_space=pltpu.VMEM)
     hbm = pl.BlockSpec(memory_space=pltpu.HBM)
+    spectrum = jax.ShapeDtypeStruct((frequencies // LANES, rows + spare, LANES), F32)
     return pl.pallas_call(
-        table_kernel,
-        out_shape=[jax.ShapeDtypeStruct(table.shape, BF16) for table in tables]
+        own_kernel,
+        out_shape=[spectrum, spectrum]
+        + [jax.ShapeDtypeStruct(table.shape, BF16) for table in tables]
         + [
             jax.ShapeDtypeStruct((WIDE, 2 * WIDE), BF16),
             jax.ShapeDtypeStruct((1, WIDE), F32),
         ],
-        in_specs=[vmem, hbm, hbm],
-        out_specs=[vmem] * 4,
+        in_specs=[vmem, vmem, hbm, hbm],
+        out_specs=[vmem] * 6,
         scratch_shapes=[pltpu.SemaphoreType.DMA((2,))],
-        compiler_params=pltpu.CompilerParams(vmem_limit_bytes=TABLE_LIMIT << 20),
-    )(taps_row, *tables)
-
-
-def own_kernel(
-    raw_ref, cos_ref, sin_ref, band_ref, scale_ref, own_cos_ref, own_sin_ref
-):
-    pieces, rows, _ = raw_ref.shape
-    even, odd = fold(
-        normalize(
-            [raw_ref[p].astype(F32) for p in range(pieces)], band_ref[...], scale_ref[...]
-        ),
-        rows,
-    )
-    spare = own_cos_ref.shape[1] - rows
-    frequencies = cos_ref.shape[1]
-    for part, table_ref, spectrum_ref in (
-        (even, cos_ref, own_cos_ref),
-        (odd, sin_ref, own_sin_ref),
-    ):
-        for start in range(0, frequencies, WIDE):
-            stop = min(start + WIDE, frequencies)
-            spectrum = jnp.dot(part, table_ref[:, start:stop], preferred_element_type=F32)
-            for lane in range(start, stop, LANES):
-                tile = spectrum[:, lane - start : lane - start + LANES]
-                spectrum_ref[lane // LANES, :rows] = tile
-                spectrum_ref[lane // LANES, rows:] = tile[:spare]
-
-
-def own_spectra(records, shared, spare):
-    rows = records.shape[1]
-    frequencies = shared[0].shape[1]
-    vmem = pl.BlockSpec(memory_space=pltpu.VMEM)
-    spectrum = jax.ShapeDtypeStruct((frequencies // LANES, rows + spare, LANES), F32)
-    return pl.pallas_call(
-        own_kernel,
-        out_shape=[spectrum, spectrum],
-        in_specs=[vmem] * (1 + len(shared)),
-        out_specs=[vmem] * 2,
         compiler_params=pltpu.CompilerParams(vmem_limit_bytes=OWN_LIMIT << 20),
-    )(records, *shared)
+    )(records, taps_row, *tables)
 
 
 def far_kernel(
@@ -163,24 +153,15 @@
     *refs,
 ):
     run_refs = refs[:3]
-    (
-        back_cos_hbm,
-        back_sin_hbm,
-        out_ref,
-        far_cos_ref,
-        far_sin_ref,
-        real_ref,
-        imag_ref,
-        back_cos_ref,
-        back_sin_ref,
-        start_ref,
-        copied,
-    ) = refs[3:]
-    start_copy = pltpu.make_async_copy(start_any, start_ref, copied.at[2])
+    back_hbms = refs[3:7]
+    out_ref, far_cos_ref, far_sin_ref = refs[7:10]
+    sum_refs, back_refs = refs[10:14], refs[14:18]
+    start_ref, copied = refs[18:]
+    start_copy = pltpu.make_async_copy(start_any, start_ref, copied.at[4])
     start_copy.start()
     copies = [
-        pltpu.make_async_copy(back_cos_hbm, back_cos_ref, copied.at[0]),
-        pltpu.make_async_copy(back_sin_hbm, back_sin_ref, copied.at[1]),
+        pltpu.make_async_copy(source, target, copied.at[place])
+        for place, (source, target) in enumerate(zip(back_hbms, back_refs))
     ]
     for copy in copies:
         copy.start()
@@ -188,7 +169,8 @@
     block_rows = share * pieces
     blocks = [(ref, place) for ref in run_refs for place in range(ref.shape[0])]
     rows = len(blocks) * share
-    frequencies = cos_ref.shape[1]
+    quarter = cos_ref.shape[1]
+    frequencies = 2 * quarter
     inside = (lax.axis_size("cable") + REACH - lax.axis_index("cable")) * share
     within = lax.broadcasted_iota(jnp.int32, (rows, run_refs[0].shape[3]), 0) < inside
     parts = [
@@ -199,15 +181,13 @@
         )
         for p in range(pieces)
     ]
-    even, odd = fold(normalize(parts, band_ref[...], scale_ref[...]), rows)
-    for start in range(0, frequencies, WIDE):
-        stop = min(start + WIDE, frequencies)
-        far_cos_ref[:, start:stop] = jnp.dot(
-            even, cos_ref[:, start:stop], preferred_element_type=F32
-        )
-        far_sin_ref[:, start:stop] = jnp.dot(
-            odd, sin_ref[:, start:stop], preferred_element_type=F32
-        )
+    for_cos, for_sin = fold(normalize(parts, band_ref[...], scale_ref[...]), rows)
+    spectrum = jnp.dot(for_cos, cos_ref[...], preferred_element_type=F32)
+    far_cos_ref[:, :quarter] = spectrum[:rows]
+    far_sin_ref[:, quarter:] = spectrum[rows:]
+    spectrum = jnp.dot(for_sin, sin_ref[...], preferred_element_type=F32)
+    far_sin_ref[:, :quarter] = spectrum[:rows]
+    far_cos_ref[:, quarter:] = spectrum[rows:]
 
     slots = start_ref.shape[0]
     first = lax.axis_index("pair") * share
@@ -227,19 +207,28 @@
         tiles = range(frequencies // LANES)
         own_cos = jnp.concatenate([own_cos_ref[tile, own] for tile in tiles], 1)
         own_sin = jnp.concatenate([own_sin_ref[tile, own] for tile in tiles], 1)
+        real = own_cos * far_cos + own_sin * far_sin
+        imag = own_cos * far_sin - own_sin * far_cos
         pair.append(
-            (own_cos * far_cos + own_sin * far_sin, own_cos * far_sin - own_sin * far_cos)
+            (
+                real[:, :quarter] + real[:, quarter:],
+                imag[:, :quarter] - imag[:, quarter:],
+                real[:, :quarter] - real[:, quarter:],
+                imag[:, :quarter] + imag[:, quarter:],
+            )
         )
         if len(pair) * share == 16:
             begin = (slot + 1) * share - 16
-            real_ref[begin : begin + 16] = jnp.concatenate([p[0] for p in pair], 0).astype(BF16)
-            imag_ref[begin : begin + 16] = jnp.concatenate([p[1] for p in pair], 0).astype(BF16)
+            for sum_ref, values in zip(sum_refs, zip(*pair)):
+                sum_ref[begin : begin + 16] = jnp.concatenate(values, 0).astype(BF16)
             pair = []
     for copy in copies:
         copy.wait()
-    result = jnp.dot(real_ref[...], back_cos_ref[...], preferred_element_type=F32) + jnp.dot(
-        imag_ref[...], back_sin_ref[...], preferred_element_type=F32
-    )
+    lag_sums = [
+        jnp.dot(sum_ref[...], back_ref[...], preferred_element_type=F32)
+        for sum_ref, back_ref in zip(sum_refs, back_refs)
+    ]
+    result = jnp.concatenate([lag_sums[0] + lag_sums[1], lag_sums[2] + lag_sums[3]], 1)
     tile = (share * LAG_PAD // LANES, LANES)
     last_lane = (lax.broadcasted_iota(jnp.int32, tile, 0) >= tile[0] - share) & (
         lax.broadcasted_iota(jnp.int32, tile, 1) == LANES - 1
@@ -262,24 +251,25 @@
     share = runs[0].shape[2]
     slots = starts.shape[0]
     rows = sum(run.shape[0] for run in runs) * share
-    frequencies = own[2].shape[1]
+    quarter = own[2].shape[1]
+    frequencies = 2 * quarter
     vmem = pl.BlockSpec(memory_space=pltpu.VMEM)
     hbm = pl.BlockSpec(memory_space=pltpu.HBM)
     anywhere = pl.BlockSpec(memory_space=pl.ANY)
     return pl.pallas_call(
         far_kernel,
         out_shape=jax.ShapeDtypeStruct((slots, share * LAG_PAD // LANES, LANES), BF16),
-        in_specs=[anywhere] + [vmem] * (len(own) + len(runs)) + [hbm] * 2,
+        in_specs=[anywhere] + [vmem] * (len(own) + len(runs)) + [hbm] * 4,
         out_specs=vmem,
         scratch_shapes=[
             pltpu.VMEM((rows, frequencies), F32),
             pltpu.VMEM((rows, frequencies), F32),
-            pltpu.VMEM((slots * share, frequencies), BF16),
-            pltpu.VMEM((slots * share, frequencies), BF16),
-            pltpu.VMEM(tables[0].shape, BF16),
-            pltpu.VMEM(tables[1].shape, BF16),
+        ]
+        + [pltpu.VMEM((slots * share, quarter), BF16)] * 4
+        + [pltpu.VMEM(table.shape, BF16) for table in tables]
+        + [
             pltpu.SMEM((slots,), jnp.int32),
-            pltpu.SemaphoreType.DMA((3,)),
+            pltpu.SemaphoreType.DMA((5,)),
         ],
         compiler_params=pltpu.CompilerParams(vmem_limit_bytes=FAR_LIMIT << 20),
     )(starts, *own, *runs, *tables)
@@ -302,14 +292,17 @@
     turn = ((ahead == 0) | (ahead == -block_rows)).astype(BF16)
     total = out_ref.shape[0]
     written = []
-    for step in range(tiles):
-        span = pl.ds(step * lanes, min(total, (step + 1) * lanes) - step * lanes)
-        out_ref[span] = lax.dot_general(
-            lags[step].astype(BF16),
-            turn,
-            (((0,), (0,)), ((), ())),
-            preferred_element_type=F32,
-        )[: span.size]
+    for step in range(tiles // 2):
+        begin, stop = 2 * step * lanes, min(total, 2 * (step + 1) * lanes)
+        for odd in (0, 1):
+            count = (stop - begin + 1 - odd) // 2
+            out_ref[pl.ds(begin + odd, count, stride=2)] = lax.dot_general(
+                lags[step + odd * tiles // 2].astype(BF16),
+                turn,
+                (((0,), (0,)), ((), ())),
+                preferred_element_type=F32,
+            )[:count]
+        span = pl.ds(begin, stop - begin)
         written.append(
             pltpu.make_async_copy(out_ref.at[span], out_hbm.at[span, 0], copied.at[step])
         )
@@ -328,7 +321,7 @@
         out_specs=hbm,
         scratch_shapes=[
             pltpu.VMEM((2 * LAG + 1, rows), F32),
-            pltpu.SemaphoreType.DMA((LAG_PAD // LANES,)),
+            pltpu.SemaphoreType.DMA((LAG_PAD // LANES // 2,)),
         ],
         compiler_params=pltpu.CompilerParams(vmem_limit_bytes=8 << 20),
     )(sent)
@@ -359,11 +352,10 @@
     lead = records.shape[2] - (smooth_taps.shape[0] - 1) // 2
     taps_row = jnp.pad(smooth_taps, (lead, 2 * WIDE - lead - smooth_taps.shape[0]))[None]
     middle, starts, taps_row = lax.optimization_barrier((middle, starts, taps_row))
-    shared = forward_tables(taps_row, tables[:2])
     lower = from_behind(middle, "cable", REACH, [(last, 1)])
     upper = from_behind(middle, "cable", -REACH)
-    own = own_spectra(records, shared, share)
-    products = far_products(starts, [*own, *shared], [lower, middle, upper], tables[2:])
+    own = own_spectra(records, taps_row, tables[:2], share)
+    products = far_products(starts, own, [lower, middle, upper], tables[2:])
     sent = lax.all_to_all(products, "pair", 0, 0)
     return place_lags(sent, rows).reshape(1, 1, 2 * LAG + 1, rows)
 

time: 62.3 us -> 62.1 us (level)
  Pallas kernels: 7.88 us -> 6 us
  waiting for transfers between devices: 3.46 us -> 4.48 us
    pallas_call x2 -> x1, Pallas kernels: 4.17 us -> 2.72 us  [own_spectra(): pl.pallas_call(own_kernel, out_shape=[spectrum, spectrum] + [jax.ShapeDty...]
    ppermute x3, waiting for transfers between devices: 3.46 us -> 4.48 us  [from_behind(): return lax.ppermute(value, axis, pairs + list(also))]
  transfers between devices with their start and end apart: 3 -> 3, of which waited for: 1 -> 2; matrix products, arithmetic and copies ran while one was open for 2% -> 2% of each run, Pallas kernels for 7% -> 4%
where the time goes in v5:
time: 62.1 us; the launch traced here: 61.8 us
  blocking collectives  39.7 us (64%)
  starting transfers between devices  9.38 us (15%)
  Pallas kernels  6 us (10%)
  waiting for transfers between devices  4.48 us (7%)
  local copies, waits for them, and re-layouts  0.77 us (1%)
  between operations  0.75 us (1%)
  other arithmetic  0.69 us (1%)
    all_gather x1, blocking collectives, per_device(): records = lax.all_gather(raw_strain, 'pair', axis=0)  25.3 us
    all_to_all x1, blocking collectives, per_device(): sent = lax.all_to_all(products, 'pair', 0, 0)  14.4 us
    ppermute x3, starting transfers between devices, from_behind(): return lax.ppermute(value, axis, pairs + list(also))  9.38 us
    ppermute x3, waiting for transfers between devices, from_behind(): return lax.ppermute(value, axis, pairs + list(also))  4.48 us
    pallas_call x1, Pallas kernels, own_spectra(): pl.pallas_call(own_kernel, out_shape=[spectrum, spectrum] + [jax.ShapeDty...  2.72 us
    pallas_call x1, Pallas kernels, far_products(): pl.pallas_call(far_kernel, out_shape=jax.ShapeDtypeStruct((slots, share *...  2.35 us
  transfers between devices with their start and end apart: 3, of which 2 were waited for; matrix products, arithmetic and copies ran while one was open for 2% of the time, Pallas kernels for 4%

profile of v5, /device:TPU:31, one launch (start us, length us, event | category | flops | bytes accessed | tf_op | source)
XLA Modules:
  0.0 61.8 jit_solution(9655611827686491832)
XLA Ops:
  0.0 25.3 %all-gather = bf16[2048,128]{1,0:T(8,128)(2,1)S(1)} all-gather(bf16[128,128]{1,0:T(8,128)(2,1)} %param.11), channel_id=2, replica_groups=mesh['cable'=32,'pair'=16] {'pair'}, dimensions={0}, use_global_device_ids=true | all-gather | bytes 557056 | tf_op jit(solution)/shard_map/all_gather | solution.py:341
  25.3 2.5 %collective-permute-start = (bf16[16,8,128]{2,1,0:T(8,128)(2,1)S(1)}, bf16[16,8,128]{2,1,0:T(8,128)(2,1)S(1)}, u32[]{:S(2)}, u32[]{:S(2)}) collective-permute-start(bf16[16,8,128]{2,1,0:T(8,128)(2,1)S(1)} %constant_dynamic-slice_fusion), channel_id=1, source_target_pairs={{16,0},{32,16},{48,32},{64,48},{80,64},{96,80},{112,96},{128,112},... | collective-permute-start | bytes 98312 | tf_op jit(solution)/shard_map/ppermute | solution.py:334
  28.5 0.7 %compare_select_fusion.start_any = s32[16]{0:T(128)S(1)} fusion(s32[1,16]{1,0:T(1,128)} %param.14, s32[1,16]{1,0:T(1,128)} %param.13, s32[]{:T(128)S(6)} %sub.10, s32[]{:T(128)} %bitcast.10), kind=kLoop, calls=%fused_computation.1 | loop fusion | flops 80 | bytes 200 | tf_op jit(solution)/shard_map/jit(_where)/select_n | solution.py:351
  29.1 0.7 %pad.4 = f32[512]{0:T(512)S(1)} pad(f32[101]{0:T(128)} %param.12, f32[]{:T(128)} %constant.34.clone.1), padding=78_333 | pad | bytes 2456 | tf_op jit(solution)/shard_map/jit(_pad)/pad | solution.py:353
  29.9 3.5 %collective-permute-done = bf16[16,8,128]{2,1,0:T(8,128)(2,1)S(1)} collective-permute-done((bf16[16,8,128]{2,1,0:T(8,128)(2,1)S(1)}, bf16[16,8,128]{2,1,0:T(8,128)(2,1)S(1)}, u32[]{:S(2)}, u32[]{:S(2)}) %collective-permute-start) | collective-permute-done | bytes 32800 | tf_op jit(solution)/shard_map/ppermute | solution.py:334
  33.3 0.0 copy-start
  33.3 0.0 copy-start.1
  33.4 0.0 copy-start.2
  33.4 0.0 copy-start.3
  33.4 2.1 %collective-permute-start.1 = (bf16[2,16,8,128]{3,2,1,0:T(8,128)(2,1)S(1)}, bf16[2,16,8,128]{3,2,1,0:T(8,128)(2,1)S(1)}, u32[]{:S(2)}, u32[]{:S(2)}) collective-permute-start(bf16[2,16,8,128]{3,2,1,0:T(8,128)(2,1)S(1)} %pad_maximum_fusion.refs_1_), channel_id=1, source_target_pairs={{0,32},{16,48},{32,64},{48,80},{64,96},{80,112},{96,128},{112,144}... | collective-permute-start | bytes 196616 | tf_op jit(solution)/shard_map/ppermute | solution.py:334
  35.5 4.8 %collective-permute-start.2 = (bf16[2,16,8,128]{3,2,1,0:T(8,128)(2,1)S(1)}, bf16[2,16,8,128]{3,2,1,0:T(8,128)(2,1)S(1)}, u32[]{:S(2)}, u32[]{:S(2)}) collective-permute-start(bf16[2,16,8,128]{3,2,1,0:T(8,128)(2,1)S(1)} %pad_maximum_fusion.refs_1_), channel_id=1, source_target_pairs={{32,0},{48,16},{64,32},{80,48},{96,64},{112,80},{128,96},{144,112}... | collective-permute-start | bytes 196616 | tf_op jit(solution)/shard_map/ppermute | solution.py:334
  40.3 2.7 %shard_map.109 = (f32[10,136,128]{2,1,0:T(8,128)S(1)}, f32[10,136,128]{2,1,0:T(8,128)S(1)}, bf16[1024,640]{1,0:T(8,128)(2,1)S(1)}, bf16[1024,640]{1,0:T(8,128)(2...) custom-call(bf16[16,128,128]{2,1,0:T(8,128)(2,1)S(1)} %bitcast.12, f32[1,512]{1,0:T(1,128)S(1)} %bitcast.13, ...), custom_call_target="tpu_custom_call" | custom-call | tf_op jit(solution)/shard_map/pallas_call | solution.py:130
  43.0 0.0 collective-permute-done.1.refs_0_
  43.1 1.0 %collective-permute-done.2.refs_2_ = bf16[2,16,8,128]{3,2,1,0:T(8,128)(2,1)S(1)} collective-permute-done((bf16[2,16,8,128]{3,2,1,0:T(8,128)(2,1)S(1)}, bf16[2,16,8,128]{3,2,1,0:T(8,128)(2,1)S(1)}, u32[]{:S(2)}, u32[]{:S(2)}) %collective-permute-start.2) | collective-permute-done | bytes 65568 | tf_op jit(solution)/shard_map/ppermute | solution.py:334
  44.1 0.0 copy-done
  44.1 0.0 copy-done.1
  44.1 0.0 copy-done.2
  44.1 0.0 copy-done.3
  44.1 2.3 %shard_map.110 = bf16[16,32,128]{2,1,0:T(8,128)(2,1)S(1)} custom-call(s32[16]{0:T(128)S(1)} %compare_select_fusion.start_any, f32[10,136,128]{2,1,0:T(8,128)S(1)} %get-tuple-element.26.own_cos_ref, f32[10,136,128]{2,1,0:T(8,128)S(1)} %get-tuple-element.27.own_sin_ref, bf16[1024,640]{1,0:T(8,128)(2,1)S(1)} %get-tuple-element.28.cos_ref, ...), custom_call_target="tpu_custom_call" | custom-call | tf_op jit(solution)/shard_map/pallas_call | solution.py:259
  46.5 14.4 %all_to_all.5.sent_ref = bf16[16,32,128]{2,1,0:T(8,128)(2,1)S(1)} all-to-all(bf16[16,32,128]{2,1,0:T(8,128)(2,1)S(1)} %shard_map.110), channel_id=1, replica_groups=mesh['cable'=32,'pair'=16] {'pair'}, dimensions={0} | all-to-all | bytes 262144 | tf_op jit(solution)/shard_map/all_to_all | solution.py:359
  60.9 0.9 %shard_map.111 = f32[401,1,128]{2,1,0:T(1,128)} custom-call(bf16[16,32,128]{2,1,0:T(8,128)(2,1)S(1)} %all_to_all.5.sent_ref), custom_call_target="tpu_custom_call" | custom-call | tf_op jit(solution)/shard_map/pallas_call | solution.py:317
  (2 shorter events, 0.0 us)
Async XLA Ops:
  25.3 8.0 %collective-permute-start = (bf16[16,8,128]{2,1,0:T(8,128)(2,1)S(1)}, bf16[16,8,128]{2,1,0:T(8,128)(2,1)S(1)}, u32[]{:S(2)}, u32[]{:S(2)}) collective-permute-start(bf16[16,8,128]{2,1,0:T(8,128)(2,1)S(1)} %constant_dynamic-slice_fusion), channel_id=1, source_target_pairs={{16,0},{32,16},{48,32},{64,48},{80,64},{96,80},{112,96},{128,112},... | collective-permute-start | bytes 98312 | tf_op jit(solution)/shard_map/ppermute | solution.py:334
  33.3 10.8 %copy-start = (bf16[640,256]{1,0:T(8,128)(2,1)S(1)}, bf16[640,256]{1,0:T(8,128)(2,1)}, u32[]{:S(2)}) copy-start(bf16[640,256]{1,0:T(8,128)(2,1)} %constant.37.clone.refs_3_) | copy-start | bytes 983044
  33.3 10.7 %copy-start.1 = (bf16[640,256]{1,0:T(8,128)(2,1)S(1)}, bf16[640,256]{1,0:T(8,128)(2,1)}, u32[]{:S(2)}) copy-start(bf16[640,256]{1,0:T(8,128)(2,1)} %constant.38.clone.refs_4_) | copy-start | bytes 983044
  33.4 10.7 %copy-start.2 = (bf16[640,256]{1,0:T(8,128)(2,1)S(1)}, bf16[640,256]{1,0:T(8,128)(2,1)}, u32[]{:S(2)}) copy-start(bf16[640,256]{1,0:T(8,128)(2,1)} %constant.39.clone.refs_5_) | copy-start | bytes 983044
  33.4 10.7 %copy-start.3 = (bf16[640,256]{1,0:T(8,128)(2,1)S(1)}, bf16[640,256]{1,0:T(8,128)(2,1)}, u32[]{:S(2)}) copy-start(bf16[640,256]{1,0:T(8,128)(2,1)} %constant.40.clone.refs_6_) | copy-start | bytes 983044
  33.4 9.7 %collective-permute-start.1 = (bf16[2,16,8,128]{3,2,1,0:T(8,128)(2,1)S(1)}, bf16[2,16,8,128]{3,2,1,0:T(8,128)(2,1)S(1)}, u32[]{:S(2)}, u32[]{:S(2)}) collective-permute-start(bf16[2,16,8,128]{3,2,1,0:T(8,128)(2,1)S(1)} %pad_maximum_fusion.refs_1_), channel_id=1, source_target_pairs={{0,32},{16,48},{32,64},{48,80},{64,96},{80,112},{96,128},{112,144}... | collective-permute-start | bytes 196616 | tf_op jit(solution)/shard_map/ppermute | solution.py:334
  35.5 8.6 %collective-permute-start.2 = (bf16[2,16,8,128]{3,2,1,0:T(8,128)(2,1)S(1)}, bf16[2,16,8,128]{3,2,1,0:T(8,128)(2,1)S(1)}, u32[]{:S(2)}, u32[]{:S(2)}) collective-permute-start(bf16[2,16,8,128]{3,2,1,0:T(8,128)(2,1)S(1)} %pad_maximum_fusion.refs_1_), channel_id=1, source_target_pairs={{32,0},{48,16},{64,32},{80,48},{96,64},{112,80},{128,96},{144,112}... | collective-permute-start | bytes 196616 | tf_op jit(solution)/shard_map/ppermute | solution.py:334

commit v6 on v5

--- a/solution.py
+++ b/solution.py
@@ -143,7 +143,9 @@
 
 
 def far_kernel(
-    start_any,
+    block_any,
+    offset_any,
+    count_ref,
     own_cos_ref,
     own_sin_ref,
     cos_ref,
@@ -156,9 +158,13 @@
     back_hbms = refs[3:7]
     out_ref, far_cos_ref, far_sin_ref = refs[7:10]
     sum_refs, back_refs = refs[10:14], refs[14:18]
-    start_ref, copied = refs[18:]
-    start_copy = pltpu.make_async_copy(start_any, start_ref, copied.at[4])
-    start_copy.start()
+    block_ref, offset_ref, copied = refs[18:]
+    slot_copies = [
+        pltpu.make_async_copy(block_any, block_ref, copied.at[4]),
+        pltpu.make_async_copy(offset_any, offset_ref, copied.at[5]),
+    ]
+    for copy in slot_copies:
+        copy.start()
     copies = [
         pltpu.make_async_copy(source, target, copied.at[place])
         for place, (source, target) in enumerate(zip(back_hbms, back_refs))
@@ -189,15 +195,16 @@
     far_sin_ref[:, :quarter] = spectrum[:rows]
     far_cos_ref[:, quarter:] = spectrum[rows:]
 
-    slots = start_ref.shape[0]
+    slots = block_ref.shape[1]
+    first_block = lax.axis_index("cable") - REACH
     first = lax.axis_index("pair") * share
     place = first + lax.broadcasted_iota(jnp.int32, (share, frequencies), 0)
     pair = []
-    start_copy.wait()
+    for copy in slot_copies:
+        copy.wait()
     for slot in range(slots):
-        start = jnp.maximum(start_ref[slot], 0)
-        block = lax.div(start, block_rows)
-        offset = lax.rem(start, block_rows)
+        block = block_ref[0, slot] - first_block
+        offset = offset_ref[0, slot]
         lower = pl.ds(pl.multiple_of(block * share, share), share)
         upper = pl.ds(pl.multiple_of(block * share + share, share), share)
         own = pl.ds(lax.rem(first - offset + block_rows, block_rows), share)
@@ -233,6 +240,7 @@
     last_lane = (lax.broadcasted_iota(jnp.int32, tile, 0) >= tile[0] - share) & (
         lax.broadcasted_iota(jnp.int32, tile, 1) == LANES - 1
     )
+    count = jnp.broadcast_to(count_ref[...], tile)
     for slot in range(slots):
         lags = jnp.concatenate(
             [
@@ -241,15 +249,14 @@
             ],
             0,
         )
-        start = start_ref[slot]
-        offset = lax.rem(jnp.maximum(start, 0), block_rows).astype(F32)
-        lags = jnp.where(start >= 0, lags, 0.0)
+        offset = offset_ref[0, slot].astype(F32)
+        lags = jnp.where(slot < count, lags, 0.0)
         out_ref[slot] = jnp.where(last_lane, offset, lags).astype(BF16)
 
 
-def far_products(starts, own, runs, tables):
+def far_products(slot_tables, own, runs, tables):
     share = runs[0].shape[2]
-    slots = starts.shape[0]
+    slots = slot_tables[0].shape[1]
     rows = sum(run.shape[0] for run in runs) * share
     quarter = own[2].shape[1]
     frequencies = 2 * quarter
@@ -259,7 +266,7 @@
     return pl.pallas_call(
         far_kernel,
         out_shape=jax.ShapeDtypeStruct((slots, share * LAG_PAD // LANES, LANES), BF16),
-        in_specs=[anywhere] + [vmem] * (len(own) + len(runs)) + [hbm] * 4,
+        in_specs=[anywhere] * 2 + [vmem] * (1 + len(own) + len(runs)) + [hbm] * 4,
         out_specs=vmem,
         scratch_shapes=[
             pltpu.VMEM((rows, frequencies), F32),
@@ -268,11 +275,12 @@
         + [pltpu.VMEM((slots * share, quarter), BF16)] * 4
         + [pltpu.VMEM(table.shape, BF16) for table in tables]
         + [
-            pltpu.SMEM((slots,), jnp.int32),
-            pltpu.SemaphoreType.DMA((5,)),
+            pltpu.SMEM((1, slots), jnp.int32),
+            pltpu.SMEM((1, slots), jnp.int32),
+            pltpu.SemaphoreType.DMA((6,)),
         ],
         compiler_params=pltpu.CompilerParams(vmem_limit_bytes=FAR_LIMIT << 20),
-    )(starts, *own, *runs, *tables)
+    )(*slot_tables, *own, *runs, *tables)
 
 
 def place_kernel(sent_ref, out_hbm, out_ref, copied):
@@ -337,25 +345,22 @@
 def per_device(raw_strain, smooth_taps, partner_block, chan_offset, pair_count):
     rows = raw_strain.shape[0]
     share = rows // lax.axis_size("pair")
-    first_block = lax.axis_index("cable") - REACH
     records = lax.all_gather(raw_strain, "pair", axis=0)
     mine = lax.dynamic_slice_in_dim(records, lax.axis_index("pair") * share, share, 1)
     tables = transform_tables(records.shape[0] * records.shape[2])
-    mine, smooth_taps, partner_block, chan_offset, pair_count = lax.optimization_barrier(
-        (mine, smooth_taps, partner_block, chan_offset, pair_count)
-    )
+    mine, smooth_taps, pair_count = lax.optimization_barrier((mine, smooth_taps, pair_count))
+    lead = records.shape[2] - (smooth_taps.shape[0] - 1) // 2
+    taps_row = jnp.pad(smooth_taps, (lead, 2 * WIDE - lead - smooth_taps.shape[0]))[None]
     last = lax.axis_size("cable") - 1
     middle = jnp.stack([mine, from_behind(mine, "cable", -1, [(0, last)])], 0)
-    starts = (partner_block[0] - first_block) * rows + chan_offset[0]
-    live = jnp.arange(starts.shape[0], dtype=jnp.int32) < pair_count
-    starts = jnp.where(live, starts, -1)
-    lead = records.shape[2] - (smooth_taps.shape[0] - 1) // 2
-    taps_row = jnp.pad(smooth_taps, (lead, 2 * WIDE - lead - smooth_taps.shape[0]))[None]
-    middle, starts, taps_row = lax.optimization_barrier((middle, starts, taps_row))
+    middle, records, taps_row, count = lax.optimization_barrier(
+        (middle, records, taps_row, pair_count[None])
+    )
     lower = from_behind(middle, "cable", REACH, [(last, 1)])
     upper = from_behind(middle, "cable", -REACH)
     own = own_spectra(records, taps_row, tables[:2], share)
-    products = far_products(starts, own, [lower, middle, upper], tables[2:])
+    slot_tables = (partner_block, chan_offset, count)
+    products = far_products(slot_tables, own, [lower, middle, upper], tables[2:])
     sent = lax.all_to_all(products, "pair", 0, 0)
     return place_lags(sent, rows).reshape(1, 1, 2 * LAG + 1, rows)
 

time: 62.1 us -> 61.9 us (level)
  other arithmetic: 0.69 us -> 0.01 us
    select_n x1 -> x0, other arithmetic: 0.68 us -> none  [per_device(): starts = jnp.where(live, starts, -1)]
  transfers between devices with their start and end apart: 3 -> 3, of which waited for: 2 -> 2; matrix products, arithmetic and copies ran while one was open for 2% -> 1% of each run, Pallas kernels for 4% -> 5%
where the time goes in v6:
time: 61.9 us; the launch traced here: 61.7 us
  blocking collectives  39.8 us (64%)
  starting transfers between devices  9.24 us (15%)
  Pallas kernels  6.1 us (10%)
  waiting for transfers between devices  5 us (8%)
  local copies, waits for them, and re-layouts  0.78 us (1%)
  between operations  0.78 us (1%)
    all_gather x1, blocking collectives, per_device(): records = lax.all_gather(raw_strain, 'pair', axis=0)  25.3 us
    all_to_all x1, blocking collectives, per_device(): sent = lax.all_to_all(products, 'pair', 0, 0)  14.4 us
    ppermute x3, starting transfers between devices, from_behind(): return lax.ppermute(value, axis, pairs + list(also))  9.24 us
    ppermute x3, waiting for transfers between devices, from_behind(): return lax.ppermute(value, axis, pairs + list(also))  5 us
    pallas_call x1, Pallas kernels, own_spectra(): pl.pallas_call(own_kernel, out_shape=[spectrum, spectrum] + [jax.ShapeDty...  2.81 us
    pallas_call x1, Pallas kernels, far_products(): pl.pallas_call(far_kernel, out_shape=jax.ShapeDtypeStruct((slots, share *...  2.37 us
  transfers between devices with their start and end apart: 3, of which 2 were waited for; matrix products, arithmetic and copies ran while one was open for 1% of the time, Pallas kernels for 5%

profile of v6, /device:TPU:31, one launch (start us, length us, event | category | flops | bytes accessed | tf_op | source)
XLA Modules:
  0.0 61.7 jit_solution(10501013645243949965)
XLA Ops:
  0.0 25.3 %all-gather = bf16[2048,128]{1,0:T(8,128)(2,1)S(1)} all-gather(bf16[128,128]{1,0:T(8,128)(2,1)} %param.11), channel_id=2, replica_groups=mesh['cable'=32,'pair'=16] {'pair'}, dimensions={0}, use_global_device_ids=true | all-gather | bytes 557056 | tf_op jit(solution)/shard_map/all_gather | solution.py:348
  25.3 2.5 %collective-permute-start = (bf16[16,8,128]{2,1,0:T(8,128)(2,1)S(1)}, bf16[16,8,128]{2,1,0:T(8,128)(2,1)S(1)}, u32[]{:S(2)}, u32[]{:S(2)}) collective-permute-start(bf16[16,8,128]{2,1,0:T(8,128)(2,1)S(1)} %constant_dynamic-slice_fusion), channel_id=1, source_target_pairs={{16,0},{32,16},{48,32},{64,48},{80,64},{96,80},{112,96},{128,112},... | collective-permute-start | bytes 98312 | tf_op jit(solution)/shard_map/ppermute | solution.py:342
  27.8 0.7 %pad.4 = f32[512]{0:T(512)S(1)} pad(f32[101]{0:T(128)} %param.12, f32[]{:T(128)} %constant.23.clone.1), padding=78_333 | pad | bytes 2456 | tf_op jit(solution)/shard_map/jit(_pad)/pad | solution.py:353
  28.5 4.8 %collective-permute-done = bf16[16,8,128]{2,1,0:T(8,128)(2,1)S(1)} collective-permute-done((bf16[16,8,128]{2,1,0:T(8,128)(2,1)S(1)}, bf16[16,8,128]{2,1,0:T(8,128)(2,1)S(1)}, u32[]{:S(2)}, u32[]{:S(2)}) %collective-permute-start) | collective-permute-done | bytes 32800 | tf_op jit(solution)/shard_map/ppermute | solution.py:342
  33.3 1.9 %collective-permute-start.1 = (bf16[2,16,8,128]{3,2,1,0:T(8,128)(2,1)S(1)}, bf16[2,16,8,128]{3,2,1,0:T(8,128)(2,1)S(1)}, u32[]{:S(2)}, u32[]{:S(2)}) collective-permute-start(bf16[2,16,8,128]{3,2,1,0:T(8,128)(2,1)S(1)} %pad_maximum_fusion.refs_1_), channel_id=1, source_target_pairs={{0,32},{16,48},{32,64},{48,80},{64,96},{80,112},{96,128},{112,144}... | collective-permute-start | bytes 196616 | tf_op jit(solution)/shard_map/ppermute | solution.py:342
  35.3 4.8 %collective-permute-start.2 = (bf16[2,16,8,128]{3,2,1,0:T(8,128)(2,1)S(1)}, bf16[2,16,8,128]{3,2,1,0:T(8,128)(2,1)S(1)}, u32[]{:S(2)}, u32[]{:S(2)}) collective-permute-start(bf16[2,16,8,128]{3,2,1,0:T(8,128)(2,1)S(1)} %pad_maximum_fusion.refs_1_), channel_id=1, source_target_pairs={{32,0},{48,16},{64,32},{80,48},{96,64},{112,80},{128,96},{144,112}... | collective-permute-start | bytes 196616 | tf_op jit(solution)/shard_map/ppermute | solution.py:342
  40.8 0.0 copy-start
  40.8 0.0 copy-start.1
  40.8 0.0 copy-start.2
  40.8 0.0 copy-start.3
  40.8 0.0 copy-start.4
  40.8 0.0 copy-start.5
  40.9 2.8 %shard_map.109 = (f32[10,136,128]{2,1,0:T(8,128)S(1)}, f32[10,136,128]{2,1,0:T(8,128)S(1)}, bf16[1024,640]{1,0:T(8,128)(2,1)S(1)}, bf16[1024,640]{1,0:T(8,128)(2...) custom-call(bf16[16,128,128]{2,1,0:T(8,128)(2,1)S(1)} %bitcast.10, f32[1,512]{1,0:T(1,128)S(1)} %bitcast.11, ...), custom_call_target="tpu_custom_call" | custom-call | tf_op jit(solution)/shard_map/pallas_call | solution.py:130
  43.7 0.0 collective-permute-done.1.refs_0_
  43.7 0.2 collective-permute-done.2.refs_2_
  43.9 0.0 copy-done
  43.9 0.0 copy-done.1
  43.9 0.0 copy-done.2
  43.9 0.0 copy-done.3
  43.9 0.0 copy-done.4
  43.9 0.0 copy-done.5
  43.9 2.4 %shard_map.110 = bf16[16,32,128]{2,1,0:T(8,128)(2,1)S(1)} custom-call(s32[1,16]{1,0:T(1,128)S(1)} %copy-done.4, s32[1,16]{1,0:T(1,128)S(1)} %copy-done.5, s32[1,1]{1,0:T(1,128)} %bitcast.8.count_ref, f32[10,136,128]{2,1,0:T(8,128)S(1)} %get-tuple-element.24.own_cos_ref, f32[10,136,128]{2,1,0:T(8,128)S(1)} %get-tuple-element.25.own_sin_ref, ...), custom_call_target="tpu_custom_call" | custom-call | tf_op jit(solution)/shard_map/pallas_call | solution.py:266
  46.3 14.4 %all_to_all.5.sent_ref = bf16[16,32,128]{2,1,0:T(8,128)(2,1)S(1)} all-to-all(bf16[16,32,128]{2,1,0:T(8,128)(2,1)S(1)} %shard_map.110), channel_id=1, replica_groups=mesh['cable'=32,'pair'=16] {'pair'}, dimensions={0} | all-to-all | bytes 262144 | tf_op jit(solution)/shard_map/all_to_all | solution.py:364
  60.8 0.9 %shard_map.111 = f32[401,1,128]{2,1,0:T(1,128)} custom-call(bf16[16,32,128]{2,1,0:T(8,128)(2,1)S(1)} %all_to_all.5.sent_ref), custom_call_target="tpu_custom_call" | custom-call | tf_op jit(solution)/shard_map/pallas_call | solution.py:325
  (2 shorter events, 0.0 us)
Async XLA Ops:
  25.3 8.0 %collective-permute-start = (bf16[16,8,128]{2,1,0:T(8,128)(2,1)S(1)}, bf16[16,8,128]{2,1,0:T(8,128)(2,1)S(1)}, u32[]{:S(2)}, u32[]{:S(2)}) collective-permute-start(bf16[16,8,128]{2,1,0:T(8,128)(2,1)S(1)} %constant_dynamic-slice_fusion), channel_id=1, source_target_pairs={{16,0},{32,16},{48,32},{64,48},{80,64},{96,80},{112,96},{128,112},... | collective-permute-start | bytes 98312 | tf_op jit(solution)/shard_map/ppermute | solution.py:342
  33.3 10.3 %collective-permute-start.1 = (bf16[2,16,8,128]{3,2,1,0:T(8,128)(2,1)S(1)}, bf16[2,16,8,128]{3,2,1,0:T(8,128)(2,1)S(1)}, u32[]{:S(2)}, u32[]{:S(2)}) collective-permute-start(bf16[2,16,8,128]{3,2,1,0:T(8,128)(2,1)S(1)} %pad_maximum_fusion.refs_1_), channel_id=1, source_target_pairs={{0,32},{16,48},{32,64},{48,80},{64,96},{80,112},{96,128},{112,144}... | collective-permute-start | bytes 196616 | tf_op jit(solution)/shard_map/ppermute | solution.py:342
  35.3 8.6 %collective-permute-start.2 = (bf16[2,16,8,128]{3,2,1,0:T(8,128)(2,1)S(1)}, bf16[2,16,8,128]{3,2,1,0:T(8,128)(2,1)S(1)}, u32[]{:S(2)}, u32[]{:S(2)}) collective-permute-start(bf16[2,16,8,128]{3,2,1,0:T(8,128)(2,1)S(1)} %pad_maximum_fusion.refs_1_), channel_id=1, source_target_pairs={{32,0},{48,16},{64,32},{80,48},{96,64},{112,80},{128,96},{144,112}... | collective-permute-start | bytes 196616 | tf_op jit(solution)/shard_map/ppermute | solution.py:342
  40.8 3.1 %copy-start = (bf16[640,256]{1,0:T(8,128)(2,1)S(1)}, bf16[640,256]{1,0:T(8,128)(2,1)}, u32[]{:S(2)}) copy-start(bf16[640,256]{1,0:T(8,128)(2,1)} %constant.26.clone.refs_3_) | copy-start | bytes 983044
  40.8 3.1 %copy-start.1 = (bf16[640,256]{1,0:T(8,128)(2,1)S(1)}, bf16[640,256]{1,0:T(8,128)(2,1)}, u32[]{:S(2)}) copy-start(bf16[640,256]{1,0:T(8,128)(2,1)} %constant.27.clone.refs_4_) | copy-start | bytes 983044
  40.8 3.1 %copy-start.2 = (bf16[640,256]{1,0:T(8,128)(2,1)S(1)}, bf16[640,256]{1,0:T(8,128)(2,1)}, u32[]{:S(2)}) copy-start(bf16[640,256]{1,0:T(8,128)(2,1)} %constant.28.clone.refs_5_) | copy-start | bytes 983044
  40.8 3.1 %copy-start.3 = (bf16[640,256]{1,0:T(8,128)(2,1)S(1)}, bf16[640,256]{1,0:T(8,128)(2,1)}, u32[]{:S(2)}) copy-start(bf16[640,256]{1,0:T(8,128)(2,1)} %constant.29.clone.refs_6_) | copy-start | bytes 983044
  40.8 3.1 %copy-start.4 = (s32[1,16]{1,0:T(1,128)S(1)}, s32[1,16]{1,0:T(1,128)}, u32[]{:S(2)}) copy-start(s32[1,16]{1,0:T(1,128)} %block_any.1) | copy-start | bytes 196
  40.8 3.1 %copy-start.5 = (s32[1,16]{1,0:T(1,128)S(1)}, s32[1,16]{1,0:T(1,128)}, u32[]{:S(2)}) copy-start(s32[1,16]{1,0:T(1,128)} %offset_any.1) | copy-start | bytes 196

commit v7 on v5

--- a/solution.py
+++ b/solution.py
@@ -171,8 +171,14 @@
     rows = len(blocks) * share
     quarter = cos_ref.shape[1]
     frequencies = 2 * quarter
-    inside = (lax.axis_size("cable") + REACH - lax.axis_index("cable")) * share
-    within = lax.broadcasted_iota(jnp.int32, (rows, run_refs[0].shape[3]), 0) < inside
+    cable = lax.axis_index("cable")
+    reverse = lax.rem(lax.div(cable, REACH), 2) == 1
+
+    def stands(block):
+        return jnp.where(reverse, 2 * REACH - block + 2 * lax.rem(block, REACH), block)
+
+    run_row = lax.broadcasted_iota(jnp.int32, (rows, run_refs[0].shape[3]), 0)
+    within = stands(lax.div(run_row, share)) < lax.axis_size("cable") + REACH - cable
     parts = [
         jnp.where(
             within,
@@ -198,8 +204,8 @@
         start = jnp.maximum(start_ref[slot], 0)
         block = lax.div(start, block_rows)
         offset = lax.rem(start, block_rows)
-        lower = pl.ds(pl.multiple_of(block * share, share), share)
-        upper = pl.ds(pl.multiple_of(block * share + share, share), share)
+        lower = pl.ds(pl.multiple_of(stands(block) * share, share), share)
+        upper = pl.ds(pl.multiple_of(stands(block + 1) * share, share), share)
         own = pl.ds(lax.rem(first - offset + block_rows, block_rows), share)
         before = place >= offset
         far_cos = jnp.where(before, far_cos_ref[lower], far_cos_ref[upper])
@@ -334,6 +340,13 @@
     return lax.ppermute(value, axis, pairs + list(also))
 
 
+def swapped(value, axis, steps, which, also=()):
+    count = lax.axis_size(axis)
+    firsts = [p for p in range(count - steps) if p // steps % 2 == which]
+    pairs = [(p, p + steps) for p in firsts] + [(p + steps, p) for p in firsts]
+    return lax.ppermute(value, axis, pairs + list(also))
+
+
 def per_device(raw_strain, smooth_taps, partner_block, chan_offset, pair_count):
     rows = raw_strain.shape[0]
     share = rows // lax.axis_size("pair")
@@ -352,10 +365,10 @@
     lead = records.shape[2] - (smooth_taps.shape[0] - 1) // 2
     taps_row = jnp.pad(smooth_taps, (lead, 2 * WIDE - lead - smooth_taps.shape[0]))[None]
     middle, starts, taps_row = lax.optimization_barrier((middle, starts, taps_row))
-    lower = from_behind(middle, "cable", REACH, [(last, 1)])
-    upper = from_behind(middle, "cable", -REACH)
+    first_swap = swapped(middle, "cable", REACH, 1, [(last, 1)])
+    second_swap = swapped(middle, "cable", REACH, 0)
     own = own_spectra(records, taps_row, tables[:2], share)
-    products = far_products(starts, own, [lower, middle, upper], tables[2:])
+    products = far_products(starts, own, [first_swap, middle, second_swap], tables[2:])
     sent = lax.all_to_all(products, "pair", 0, 0)
     return place_lags(sent, rows).reshape(1, 1, 2 * LAG + 1, rows)
 

time: 62.1 us -> 61.6 us (level)
  the two profiles are of different devices: /device:TPU:31 before, /device:TPU:35 now
where the time goes in v7:
time: 61.6 us; the launch traced here: 61.4 us
  blocking collectives  39.7 us (64%)
  starting transfers between devices  11.2 us (18%)
  Pallas kernels  5.99 us (10%)
  waiting for transfers between devices  2.28 us (4%)
  local copies, waits for them, and re-layouts  0.77 us (1%)
  between operations  0.75 us (1%)
  other arithmetic  0.69 us (1%)
    all_gather x1, blocking collectives, per_device(): records = lax.all_gather(raw_strain, 'pair', axis=0)  25.3 us
    all_to_all x1, blocking collectives, per_device(): sent = lax.all_to_all(products, 'pair', 0, 0)  14.4 us
    ppermute x2, starting transfers between devices, swapped(): return lax.ppermute(value, axis, pairs + list(also))  9.01 us
    pallas_call x1, Pallas kernels, own_spectra(): pl.pallas_call(own_kernel, out_shape=[spectrum, spectrum] + [jax.ShapeDty...  2.72 us
    pallas_call x1, Pallas kernels, far_products(): pl.pallas_call(far_kernel, out_shape=jax.ShapeDtypeStruct((slots, share *...  2.34 us
    ppermute x1, starting transfers between devices, from_behind(): return lax.ppermute(value, axis, pairs + list(also))  2.16 us
    ppermute x2, waiting for transfers between devices, swapped(): return lax.ppermute(value, axis, pairs + list(also))  1.85 us
  transfers between devices with their start and end apart: 3, of which 2 were waited for; matrix products, arithmetic and copies ran while one was open for 2% of the time, Pallas kernels for 4%

profile of v7, /device:TPU:35, one launch (start us, length us, event | category | flops | bytes accessed | tf_op | source)
XLA Modules:
  0.0 61.4 jit_solution(8061755391764696965)
XLA Ops:
  0.0 25.3 %all-gather = bf16[2048,128]{1,0:T(8,128)(2,1)S(1)} all-gather(bf16[128,128]{1,0:T(8,128)(2,1)} %param.11), channel_id=2, replica_groups=mesh['cable'=32,'pair'=16] {'pair'}, dimensions={0}, use_global_device_ids=true | all-gather | bytes 557056 | tf_op jit(solution)/shard_map/all_gather | solution.py:354
  25.3 2.2 %collective-permute-start = (bf16[16,8,128]{2,1,0:T(8,128)(2,1)S(1)}, bf16[16,8,128]{2,1,0:T(8,128)(2,1)S(1)}, u32[]{:S(2)}, u32[]{:S(2)}) collective-permute-start(bf16[16,8,128]{2,1,0:T(8,128)(2,1)S(1)} %constant_dynamic-slice_fusion), channel_id=1, source_target_pairs={{16,0},{32,16},{48,32},{64,48},{80,64},{96,80},{112,96},{128,112},... | collective-permute-start | bytes 98312 | tf_op jit(solution)/shard_map/ppermute | solution.py:340
  28.2 0.7 %compare_select_fusion.start_any = s32[16]{0:T(128)S(1)} fusion(s32[1,16]{1,0:T(1,128)} %param.14, s32[1,16]{1,0:T(1,128)} %param.13, s32[]{:T(128)S(6)} %sub.10, s32[]{:T(128)} %bitcast.10), kind=kLoop, calls=%fused_computation.1 | loop fusion | flops 80 | bytes 200 | tf_op jit(solution)/shard_map/jit(_where)/select_n | solution.py:364
  28.8 0.7 %pad.4 = f32[512]{0:T(512)S(1)} pad(f32[101]{0:T(128)} %param.12, f32[]{:T(128)} %constant.34.clone.1), padding=78_333 | pad | bytes 2456 | tf_op jit(solution)/shard_map/jit(_pad)/pad | solution.py:366
  29.6 0.4 collective-permute-done
  30.0 0.0 copy-start
  30.0 0.0 copy-start.1
  30.0 0.0 copy-start.2
  30.1 0.0 copy-start.3
  30.1 7.1 %collective-permute-start.1 = (bf16[2,16,8,128]{3,2,1,0:T(8,128)(2,1)S(1)}, bf16[2,16,8,128]{3,2,1,0:T(8,128)(2,1)S(1)}, u32[]{:S(2)}, u32[]{:S(2)}) collective-permute-start(bf16[2,16,8,128]{3,2,1,0:T(8,128)(2,1)S(1)} %pad_maximum_fusion.refs_1_), channel_id=1, source_target_pairs={{32,64},{48,80},{96,128},{112,144},{160,192},{176,208},{224,256},{... | collective-permute-start | bytes 196616 | tf_op jit(solution)/shard_map/ppermute | solution.py:347
  37.2 1.9 %collective-permute-start.2 = (bf16[2,16,8,128]{3,2,1,0:T(8,128)(2,1)S(1)}, bf16[2,16,8,128]{3,2,1,0:T(8,128)(2,1)S(1)}, u32[]{:S(2)}, u32[]{:S(2)}) collective-permute-start(bf16[2,16,8,128]{3,2,1,0:T(8,128)(2,1)S(1)} %pad_maximum_fusion.refs_1_), channel_id=1, source_target_pairs={{0,32},{16,48},{64,96},{80,112},{128,160},{144,176},{192,224},{208... | collective-permute-start | bytes 196616 | tf_op jit(solution)/shard_map/ppermute | solution.py:347
  39.1 2.7 %shard_map.109 = (f32[10,136,128]{2,1,0:T(8,128)S(1)}, f32[10,136,128]{2,1,0:T(8,128)S(1)}, bf16[1024,640]{1,0:T(8,128)(2,1)S(1)}, bf16[1024,640]{1,0:T(8,128)(2...) custom-call(bf16[16,128,128]{2,1,0:T(8,128)(2,1)S(1)} %bitcast.12, f32[1,512]{1,0:T(1,128)S(1)} %bitcast.13, ...), custom_call_target="tpu_custom_call" | custom-call | tf_op jit(solution)/shard_map/pallas_call | solution.py:130
  41.8 0.0 collective-permute-done.1.refs_0_
  41.8 1.8 %collective-permute-done.2.refs_2_ = bf16[2,16,8,128]{3,2,1,0:T(8,128)(2,1)S(1)} collective-permute-done((bf16[2,16,8,128]{3,2,1,0:T(8,128)(2,1)S(1)}, bf16[2,16,8,128]{3,2,1,0:T(8,128)(2,1)S(1)}, u32[]{:S(2)}, u32[]{:S(2)}) %collective-permute-start.2) | collective-permute-done | bytes 65568 | tf_op jit(solution)/shard_map/ppermute | solution.py:347
  43.7 0.0 copy-done
  43.7 0.0 copy-done.1
  43.7 0.0 copy-done.2
  43.7 0.0 copy-done.3
  43.7 2.3 %shard_map.110 = bf16[16,32,128]{2,1,0:T(8,128)(2,1)S(1)} custom-call(s32[16]{0:T(128)S(1)} %compare_select_fusion.start_any, f32[10,136,128]{2,1,0:T(8,128)S(1)} %get-tuple-element.26.own_cos_ref, f32[10,136,128]{2,1,0:T(8,128)S(1)} %get-tuple-element.27.own_sin_ref, bf16[1024,640]{1,0:T(8,128)(2,1)S(1)} %get-tuple-element.28.cos_ref, ...), custom_call_target="tpu_custom_call" | custom-call | tf_op jit(solution)/shard_map/pallas_call | solution.py:265
  46.0 14.4 %all_to_all.5.sent_ref = bf16[16,32,128]{2,1,0:T(8,128)(2,1)S(1)} all-to-all(bf16[16,32,128]{2,1,0:T(8,128)(2,1)S(1)} %shard_map.110), channel_id=1, replica_groups=mesh['cable'=32,'pair'=16] {'pair'}, dimensions={0} | all-to-all | bytes 262144 | tf_op jit(solution)/shard_map/all_to_all | solution.py:372
  60.5 0.9 %shard_map.111 = f32[401,1,128]{2,1,0:T(1,128)} custom-call(bf16[16,32,128]{2,1,0:T(8,128)(2,1)S(1)} %all_to_all.5.sent_ref), custom_call_target="tpu_custom_call" | custom-call | tf_op jit(solution)/shard_map/pallas_call | solution.py:323
  (2 shorter events, 0.0 us)
Async XLA Ops:
  25.3 4.7 %collective-permute-start = (bf16[16,8,128]{2,1,0:T(8,128)(2,1)S(1)}, bf16[16,8,128]{2,1,0:T(8,128)(2,1)S(1)}, u32[]{:S(2)}, u32[]{:S(2)}) collective-permute-start(bf16[16,8,128]{2,1,0:T(8,128)(2,1)S(1)} %constant_dynamic-slice_fusion), channel_id=1, source_target_pairs={{16,0},{32,16},{48,32},{64,48},{80,64},{96,80},{112,96},{128,112},... | collective-permute-start | bytes 98312 | tf_op jit(solution)/shard_map/ppermute | solution.py:340
  30.0 13.7 %copy-start = (bf16[640,256]{1,0:T(8,128)(2,1)S(1)}, bf16[640,256]{1,0:T(8,128)(2,1)}, u32[]{:S(2)}) copy-start(bf16[640,256]{1,0:T(8,128)(2,1)} %constant.37.clone.refs_3_) | copy-start | bytes 983044
  30.0 13.7 %copy-start.1 = (bf16[640,256]{1,0:T(8,128)(2,1)S(1)}, bf16[640,256]{1,0:T(8,128)(2,1)}, u32[]{:S(2)}) copy-start(bf16[640,256]{1,0:T(8,128)(2,1)} %constant.38.clone.refs_4_) | copy-start | bytes 983044
  30.0 13.6 %copy-start.2 = (bf16[640,256]{1,0:T(8,128)(2,1)S(1)}, bf16[640,256]{1,0:T(8,128)(2,1)}, u32[]{:S(2)}) copy-start(bf16[640,256]{1,0:T(8,128)(2,1)} %constant.39.clone.refs_5_) | copy-start | bytes 983044
  30.1 13.6 %copy-start.3 = (bf16[640,256]{1,0:T(8,128)(2,1)S(1)}, bf16[640,256]{1,0:T(8,128)(2,1)}, u32[]{:S(2)}) copy-start(bf16[640,256]{1,0:T(8,128)(2,1)} %constant.40.clone.refs_6_) | copy-start | bytes 983044
  30.1 11.8 %collective-permute-start.1 = (bf16[2,16,8,128]{3,2,1,0:T(8,128)(2,1)S(1)}, bf16[2,16,8,128]{3,2,1,0:T(8,128)(2,1)S(1)}, u32[]{:S(2)}, u32[]{:S(2)}) collective-permute-start(bf16[2,16,8,128]{3,2,1,0:T(8,128)(2,1)S(1)} %pad_maximum_fusion.refs_1_), channel_id=1, source_target_pairs={{32,64},{48,80},{96,128},{112,144},{160,192},{176,208},{224,256},{... | collective-permute-start | bytes 196616 | tf_op jit(solution)/shard_map/ppermute | solution.py:347
  37.2 6.5 %collective-permute-start.2 = (bf16[2,16,8,128]{3,2,1,0:T(8,128)(2,1)S(1)}, bf16[2,16,8,128]{3,2,1,0:T(8,128)(2,1)S(1)}, u32[]{:S(2)}, u32[]{:S(2)}) collective-permute-start(bf16[2,16,8,128]{3,2,1,0:T(8,128)(2,1)S(1)} %pad_maximum_fusion.refs_1_), channel_id=1, source_target_pairs={{0,32},{16,48},{64,96},{80,112},{128,160},{144,176},{192,224},{208... | collective-permute-start | bytes 196616 | tf_op jit(solution)/shard_map/ppermute | solution.py:347
